TPU v7x, 32 devices: a whole 2x2x4 slice. The times are simulated.
32 devices in a mesh: high: 4 (over y, core), mid: 8 (over z, x).
Axes of the slice: x: 2, y: 2, z: 4, core: 2. Of those that a mesh axis runs over, the one named last changes fastest.
Arguments:
- amplitudes: float32 [2, 4, 8, 524288], P(None, 'high', 'mid'), may hold values from -6 to 6
- layer_gates: float32 [4, 2, 128, 128], replicated, may hold values from -0.375 to 0.375
- ctrl_gate: float32 [2, 64, 64], replicated, may hold values from -0.5 to 0.5
- control_mask: int32 [4, 8, 8192], P('high', 'mid'), may hold values 0 or 1
- mid_angles: float32 [3], replicated, may hold values from -3.140625 to 3.140625
Outputs:
- final_state: float32 [2, 4, 8, 524288], P(None, 'high', 'mid')
All inputs are finite; a program needn't handle non-finite values. No bound on the sum of `control_mask` on one device may be relied on, other than what follows from the above.
Results may differ from a plain program's by a relative error of at most 0.0003.
Values sent between devices are 32-bit elements; how exact they have to be, the bound alone decides.
No kernel may reach another device: no remote copies, remote signals or barrier semaphores. Data moves between devices by JAX's collectives and lax.ppermute only.
A program may use at most 64 MiB of HBM per device.

v0:
```python
import functools

import jax
import jax.numpy as jnp
from jax import lax
from jax.experimental import pallas as pl
from jax.experimental.pallas import tpu as pltpu
from jax.sharding import PartitionSpec as P

LANES = 128
HALF = 64
VMEM_LIMIT = 48 * 1024 * 1024
COST = pl.CostEstimate(flops=1, bytes_accessed=1, transcendentals=0)


def split_two(value):
    high = value.astype(jnp.bfloat16)
    low = (value - high.astype(jnp.float32)).astype(jnp.bfloat16)
    return high, low


def matmul(left, right):
    return lax.dot_general(left, right, (((1,), (0,)), ((), ())), preferred_element_type=jnp.float32)


def matmul_nt(left, right):
    return lax.dot_general(left, right, (((1,), (1,)), ((), ())), preferred_element_type=jnp.float32)


def right_gate(value, gate_high, gate_low):
    high, low = split_two(value)
    return matmul_nt(high, gate_high) + (matmul_nt(low, gate_high) + matmul_nt(high, gate_low))


def times_i(value):
    lane = lax.broadcasted_iota(jnp.int32, value.shape, 1)
    turned = pltpu.roll(value, HALF, 1)
    return jnp.where(lane < HALF, -turned, turned)


def left_operand(gate_ref):
    real_high, real_low = split_two(gate_ref[0, 0])
    imag_high, imag_low = split_two(gate_ref[0, 1])
    empty = jnp.zeros_like(real_low)
    return jnp.concatenate(
        [
            jnp.concatenate([real_high, real_high], axis=1),
            jnp.concatenate([imag_high, imag_high], axis=1),
            jnp.concatenate([real_low, empty], axis=1),
            jnp.concatenate([imag_low, empty], axis=1),
        ],
        axis=0,
    )


def left_gate(gate, value):
    product = matmul(gate, jnp.concatenate(split_two(value), axis=0))
    real = product[:LANES] + product[2 * LANES : 3 * LANES]
    imag = product[LANES : 2 * LANES] + product[3 * LANES :]
    return [
        real[:, begin : begin + LANES] + times_i(imag[:, begin : begin + LANES]) for begin in (0, LANES)
    ]


def early_kernel(blocks, tail, who_ref, x_ref, gate_a_ref, gate_b_ref, mask_ref, *refs):
    part_ref, zero_ref, one_ref, wide_high, wide_low, left = refs[-6:]
    step = pl.program_id(0)
    rows = blocks * LANES

    @pl.when(step == 0)
    def _():
        real, imag = gate_a_ref[0, 0], gate_a_ref[0, 1]
        pieces = []
        for begin in (0, HALF):
            piece_real, piece_imag = real[begin : begin + HALF], imag[begin : begin + HALF]
            pieces.append(jnp.concatenate([piece_real, -piece_imag], axis=1))
            pieces.append(jnp.concatenate([piece_imag, piece_real], axis=1))
        wide_high[...], wide_low[...] = split_two(jnp.concatenate(pieces, axis=0))
        left[...] = left_operand(gate_b_ref)
        if tail:
            mask = mask_ref[...].astype(jnp.float32)
            begin = part_ref.shape[0] - tail
            part_ref[pl.ds(begin, tail // 2)] = mask[:, :LANES]
            part_ref[pl.ds(begin + tail // 2, tail // 2)] = mask[:, LANES:]

    value = jnp.concatenate([x_ref[part, 0].reshape(rows, LANES) for part in range(2)], axis=1)
    value = right_gate(value, wide_high[...], wide_low[...])
    for block in range(blocks):
        zero, one = left_gate(left[...], value[block * LANES : (block + 1) * LANES])
        part_ref[pl.ds(pl.multiple_of(step * rows, rows) + block * LANES, LANES)] = zero
        zero_ref[0, pl.ds(block * LANES, LANES)] = zero
        one_ref[0, pl.ds(block * LANES, LANES)] = one


def early(who, x, gates, mask, apart, carried):
    groups, blocks = x.shape[1], x.shape[2]
    rows = blocks * LANES
    steps = 2 if blocks % 2 == 0 else 1
    tail = 2 * mask.shape[0] if apart == 0 else 0
    full = jax.ShapeDtypeStruct((groups, rows, LANES), jnp.float32)
    full_spec = pl.BlockSpec((1, rows // steps, LANES), lambda g, who: (who[0] ^ apart, g, 0))
    return pl.pallas_call(
        functools.partial(early_kernel, blocks // steps, tail),
        grid_spec=pltpu.PrefetchScalarGridSpec(
            num_scalar_prefetch=1,
            grid=(steps,),
            in_specs=[
                pl.BlockSpec((2, 1, blocks // steps, LANES, LANES), lambda g, who: (0, who[0] ^ apart, g, 0, 0)),
                pl.BlockSpec((1, 2, LANES, LANES), lambda g, who: (0, 0, 0, 0)),
                pl.BlockSpec((1, 2, LANES, LANES), lambda g, who: (1, 0, 0, 0)),
                pl.BlockSpec(mask.shape, lambda g, who: (0, 0)),
            ]
            + [pl.BlockSpec(memory_space=pl.ANY)] * len(carried),
            out_specs=[pl.BlockSpec((rows + tail, LANES), lambda g, who: (0, 0)), full_spec, full_spec],
            scratch_shapes=[
                pltpu.VMEM((2 * LANES, 2 * LANES), jnp.bfloat16),
                pltpu.VMEM((2 * LANES, 2 * LANES), jnp.bfloat16),
                pltpu.VMEM((4 * LANES, 2 * LANES), jnp.bfloat16),
            ],
        ),
        out_shape=[jax.ShapeDtypeStruct((rows + tail, LANES), jnp.float32), full, full],
        input_output_aliases={5: 1, 6: 2} if carried else {},
        compiler_params=pltpu.CompilerParams(vmem_limit_bytes=VMEM_LIMIT),
        cost_estimate=COST,
        name="early",
    )(who, x, gates, gates, mask, *carried)


def mix(coef_ref, at, value):
    return coef_ref[at] * value + coef_ref[at + 1] * times_i(value)


def late_kernel(half, parts, outs, *refs):
    sources = refs[:parts]
    gate_a_ref, gate_b_ref, ctrl_ref = refs[parts : parts + 3]
    held, control, left_a, left_b, right = refs[-5:]
    targets = refs[-5 - outs : -5]
    extra = refs[parts + 3 : -5 - outs]
    total = held.shape[0]
    stride = total // LANES

    left_a[...] = left_operand(gate_a_ref)
    left_b[...] = left_operand(gate_b_ref)
    high, low = split_two(ctrl_ref[...])
    right[...] = jnp.concatenate(
        [jnp.concatenate([high, high], axis=1), jnp.concatenate([low, jnp.zeros_like(low)], axis=1)], axis=0
    )
    if parts == 1:
        control[...] = extra[0][...].astype(jnp.float32)
        held[...] = sources[0][...]
    else:
        who_ref, own_ref, coef_ref = extra
        rows = total // parts
        tail = control.shape[0]
        control[:, :LANES] = sources[0][pl.ds(rows, tail), :]
        control[:, LANES:] = sources[0][pl.ds(rows + tail, tail), :]
        for apart in range(parts):
            held[pl.ds(pl.multiple_of((who_ref[0] ^ apart) * rows, rows), rows), :] = sources[apart][pl.ds(0, rows), :]

    @pl.loop(0, stride // 4)
    def _(step):
        for pair in range(2):
            first = step * 4 + pair * 2
            places = [pl.ds(first + side, LANES, stride=stride) for side in range(2)]
            value = jnp.concatenate([held[place, :] for place in places], axis=1)
            for place, piece in zip(places, left_gate(left_a[...], value)):
                held[place, :] = piece

    blocks = 4
    here = lax.broadcasted_iota(jnp.int32, (LANES, 2 * LANES), 0)
    there = lax.broadcasted_iota(jnp.int32, (LANES, 2 * LANES), 1)
    picked = there == 2 * here + half
    ones = jnp.ones((2 * LANES, LANES), jnp.bfloat16)
    span = total // outs

    for out in range(outs):
        target = targets[out]

        @pl.loop(0, span // (blocks * LANES))
        def _(step):
            begin = pl.multiple_of(step * (blocks * LANES), blocks * LANES)
            value = held[pl.ds(out * span + begin, blocks * LANES), :]
            acted = matmul_nt(jnp.concatenate(split_two(value), axis=1), right[...])
            acted = acted[:, :LANES] + acted[:, LANES:]
            chosen = []
            for block in range(blocks):
                row = control[pl.ds(out * (span // LANES) + step * blocks + block, 1), :]
                chosen.append(jnp.where(picked, jnp.broadcast_to(row, picked.shape), 0.0))
            chosen = matmul(jnp.concatenate(chosen, axis=0).astype(jnp.bfloat16), ones)
            value = jnp.where(chosen > 0.5, acted, value)
            for block in range(0, blocks, 2):
                both = jnp.concatenate(
                    [value[(block + side) * LANES : (block + side + 1) * LANES] for side in range(2)], axis=1
                )
                for side, piece in enumerate(left_gate(left_b[...], both)):
                    place = pl.ds(begin + (block + side) * LANES, LANES)
                    if parts > 1:
                        piece = mix(coef_ref, 0, own_ref[place, :]) + mix(coef_ref, 2, piece)
                    target[place, :] = piece


def late(sources, gates, ctrl, half, outs, *extra):
    parts = len(sources)
    total = sources[-1].shape[0] * parts
    vmem = pl.BlockSpec(memory_space=pltpu.VMEM)
    smem = pl.BlockSpec(memory_space=pltpu.SMEM)
    gate_specs = [pl.BlockSpec((1, 2, LANES, LANES), lambda g, at=at: (at, 0, 0, 0)) for at in (2, 3)]
    return pl.pallas_call(
        functools.partial(late_kernel, half, parts, outs),
        grid=(1,),
        in_specs=[vmem] * parts + gate_specs + [vmem] + ([vmem] if parts == 1 else [smem, vmem, smem]),
        out_specs=[vmem] * outs,
        out_shape=[jax.ShapeDtypeStruct((total // outs, LANES), jnp.float32)] * outs,
        scratch_shapes=[
            pltpu.VMEM((total, LANES), jnp.float32),
            pltpu.VMEM((total // LANES, 2 * LANES), jnp.float32),
            pltpu.VMEM((4 * LANES, 2 * LANES), jnp.bfloat16),
            pltpu.VMEM((4 * LANES, 2 * LANES), jnp.bfloat16),
            pltpu.VMEM((2 * LANES, 2 * LANES), jnp.bfloat16),
        ],
        compiler_params=pltpu.CompilerParams(vmem_limit_bytes=VMEM_LIMIT),
        cost_estimate=COST,
        name="late",
    )(*sources, gates, gates, ctrl, *extra)


def final_kernel(zero_ref, own_ref, other_ref, coef_ref, *refs):
    out_ref = refs[-1]
    zero = zero_ref[...]
    one = mix(coef_ref, 0, own_ref[...]) + mix(coef_ref, 2, other_ref[...])
    lane = lax.broadcasted_iota(jnp.int32, zero.shape, 1)
    out_ref[0] = jnp.where(lane < HALF, zero, pltpu.roll(one, HALF, 1))
    out_ref[1] = jnp.where(lane < HALF, pltpu.roll(zero, HALF, 1), one)


def final(zero, own, other, coefs, part, carried):
    total, rows = zero.shape[0], own.shape[0]
    steps = 2
    size = rows // steps
    here = pl.BlockSpec((size, LANES), lambda g: (g, 0))
    return pl.pallas_call(
        final_kernel,
        grid=(steps,),
        in_specs=[
            pl.BlockSpec((size, LANES), lambda g: (part * steps + g, 0)),
            here,
            here,
            pl.BlockSpec(memory_space=pltpu.SMEM),
        ]
        + [pl.BlockSpec(memory_space=pl.ANY)] * len(carried),
        out_specs=pl.BlockSpec((2, size, LANES), lambda g: (0, part * steps + g, 0)),
        out_shape=jax.ShapeDtypeStruct((2, total, LANES), jnp.float32),
        input_output_aliases={4: 0} if carried else {},
        compiler_params=pltpu.CompilerParams(vmem_limit_bytes=VMEM_LIMIT),
        cost_estimate=COST,
        name="final",
    )(zero, own, other, coefs, *carried)


def coefficients(mid_angles, parity):
    cosine, sine = jnp.cos(mid_angles), jnp.sin(mid_angles)
    sign = (1 - 2 * parity).astype(jnp.float32)
    return jnp.stack(
        [cosine[0] * cosine[1], sign * (cosine[0] * sine[1]), -sign * (sine[0] * cosine[2]), -sine[0] * sine[2]]
    )


def wide_ctrl(ctrl_gate):
    return jnp.block([[ctrl_gate[0], -ctrl_gate[1]], [ctrl_gate[1], ctrl_gate[0]]])


def body(amplitudes, layer_gates, ctrl_gate, control_mask, mid_angles):
    amount = amplitudes.shape[-1]
    total = amount // LANES
    groups = lax.axis_size("high")
    mid = lax.axis_size("mid")
    top_bit = mid.bit_length() - 2
    parity = lax.axis_index("mid") >> top_bit & 1
    who = lax.axis_index("high").astype(jnp.int32).reshape(1)

    def partner(value, apart=0):
        pairs = [
            (high * mid + at, (high ^ apart) * mid + (at ^ 1 << top_bit)) for high in range(groups) for at in range(mid)
        ]
        return lax.ppermute(value, ("high", "mid"), pairs)

    def trade(value):
        return lax.all_to_all(value, "high", split_axis=0, concat_axis=0, tiled=True).reshape(total, LANES)

    x = amplitudes.reshape(2, groups, total // groups // LANES, LANES, LANES)
    mask = control_mask.reshape(total // LANES, 2 * LANES)
    carried, away = (), []
    for apart in range(groups):
        part, *carried = early(who, x, layer_gates, mask, apart, carried)
        away.append(partner(part, apart))
    zero, one = carried
    ctrl = wide_ctrl(ctrl_gate)
    coefs = coefficients(mid_angles, parity)
    outs = 4
    one = trade(one)
    own_one = late([one], layer_gates, ctrl, 1, outs, mask)
    other_one = [partner(piece) for piece in own_one]
    zero, _ = lax.optimization_barrier((zero, one))
    (own_zero,) = late([trade(zero)], layer_gates, ctrl, 0, 1, mask)
    (mixed,) = late(away, layer_gates, ctrl, 0, 1, who, own_zero, coefs)
    result = ()
    for at in range(outs):
        result = (final(mixed, own_one[at], other_one[at], coefs, at, result),)
    return result[0].reshape(2, 1, 1, amount)


def solution(mesh):
    placed = (P(None, "high", "mid", None), P(), P(), P("high", "mid", None), P())
    return jax.shard_map(
        body, mesh=mesh, in_specs=placed, out_specs=P(None, "high", "mid", None), check_vma=False
    )
```

profile of v0, /device:TPU:0, one launch (start us, length us, event | category | flops | bytes accessed | tf_op | source)
XLA Modules:
  0.0 245.0 jit_solution(5037939095461941613)
XLA Ops:
  0.5 1.5 reduce.3
  2.0 1.0 copy-done
  3.1 4.2 %early.4 = (f32[1088,128]{1,0:T(8,128)S(1)}, f32[4,1024,128]{2,1,0:T(8,128)}, f32[4,1024,128]{2,1,0:T(8,128)S(1)}) custom-call(s32[1]{0:T(128)} %bitcast.who_ref.refs_7_, f32[2,4,8,128,128]{4,3,2,1,0:T(8,128)} %bitcast.16, f32[4,2,128,128]{3,2,1,0:T(8,128)S(1)} %copy-done, f32[4,2,128,128]{3,2,1,0:T(8,128)S(1)} %copy-done, ...), custom_call_target="tpu_custom_call" | custom-call | flops 1 | bytes 1 | tf_op jit(solution)/shard_map/early/pallas_call | solution.py:102
  7.3 0.8 copy-done.9
  8.1 4.4 %early.5 = (f32[1024,128]{1,0:T(8,128)}, f32[4,1024,128]{2,1,0:T(8,128)}, f32[4,1024,128]{2,1,0:T(8,128)S(1)}) custom-call(s32[1]{0:T(128)} %bitcast.who_ref.refs_7_, f32[2,4,8,128,128]{4,3,2,1,0:T(8,128)} %bitcast.17, f32[4,2,128,128]{3,2,1,0:T(8,128)S(1)} %copy-done, f32[4,2,128,128]{3,2,1,0:T(8,128)S(1)} %copy-done, ...), custom_call_target="tpu_custom_call", output_to_operand_aliasing={{1}: (5, {}), {2}: (6, {})} | custom-call | flops 1 | bytes 1 | tf_op jit(solution)/shard_map/early/pallas_call | solution.py:102
  12.5 4.4 %early.6 = (f32[1024,128]{1,0:T(8,128)}, f32[4,1024,128]{2,1,0:T(8,128)}, f32[4,1024,128]{2,1,0:T(8,128)S(1)}) custom-call(s32[1]{0:T(128)} %bitcast.who_ref.refs_7_, f32[2,4,8,128,128]{4,3,2,1,0:T(8,128)} %bitcast.18, f32[4,2,128,128]{3,2,1,0:T(8,128)S(1)} %copy-done, f32[4,2,128,128]{3,2,1,0:T(8,128)S(1)} %copy-done, ...), custom_call_target="tpu_custom_call", output_to_operand_aliasing={{1}: (5, {}), {2}: (6, {})} | custom-call | flops 1 | bytes 1 | tf_op jit(solution)/shard_map/early/pallas_call | solution.py:102
  16.9 4.4 %early.7 = (f32[1024,128]{1,0:T(8,128)}, f32[4,1024,128]{2,1,0:T(8,128)}, f32[4,1024,128]{2,1,0:T(8,128)S(1)}) custom-call(s32[1]{0:T(128)} %bitcast.who_ref.refs_7_, f32[2,4,8,128,128]{4,3,2,1,0:T(8,128)} %bitcast.19, f32[4,2,128,128]{3,2,1,0:T(8,128)S(1)} %copy-done, f32[4,2,128,128]{3,2,1,0:T(8,128)S(1)} %copy-done, ...), custom_call_target="tpu_custom_call", output_to_operand_aliasing={{1}: (5, {}), {2}: (6, {})} | custom-call | flops 1 | bytes 1 | tf_op jit(solution)/shard_map/early/pallas_call | solution.py:102
  21.3 29.7 %all_to_all.10 = f32[4,1024,128]{2,1,0:T(8,128)S(1)} all-to-all(f32[4,1024,128]{2,1,0:T(8,128)S(1)} %get-tuple-element.33), channel_id=1, replica_groups=mesh['high'=4,'mid'=8] {'high'}, dimensions={0} | all-to-all | bytes 4194304 | tf_op jit(solution)/shard_map/all_to_all | solution.py:288
  51.1 4.6 %all-to-all-start.1 = ((f32[4,1024,128]{2,1,0:T(8,128)}), f32[4,1024,128]{2,1,0:T(8,128)}, u32[]{:S(2)}, u32[]{:S(2)}) async-start(f32[4,1024,128]{2,1,0:T(8,128)} %get-tuple-element.34), calls=%async_computation.1 | async-start | bytes 4194304 | tf_op jit(solution)/shard_map/all_to_all | solution.py:288
  55.7 3.7 %collective-permute-start.3 = (f32[1024,128]{1,0:T(8,128)}, f32[1024,128]{1,0:T(8,128)S(1)}, u32[]{:S(2)}, u32[]{:S(2)}) collective-permute-start(f32[1024,128]{1,0:T(8,128)} %get-tuple-element.31), channel_id=1, source_target_pairs={{0,28},{1,29},{2,30},{3,31},{4,24},{5,25},{6,26},{7,27},{8,20},{9,... | collective-permute-start | bytes 1572872 | tf_op jit(solution)/shard_map/ppermute | solution.py:285
  59.7 1.9 collective-permute-start.1
  61.6 0.7 collective-permute-start
  62.4 11.5 %late.5 = (f32[1024,128]{1,0:T(8,128)}, f32[1024,128]{1,0:T(8,128)}, f32[1024,128]{1,0:T(8,128)}, f32[1024,128]{1,0:T(8,128)}) custom-call(f32[4096,128]{1,0:T(8,128)S(1)} %bitcast.15, f32[4,2,128,128]{3,2,1,0:T(8,128)S(1)} %copy-done.1, f32[4,2,128,128]{3,2,1,0:T(8,128)S(1)} %copy-done.1, f32[128,128]{1,0:T(8,128)S(1)} %maximum_maximum_fusion.refs_3_.refs_6_, ...), custom_call_target="tpu_custom_call" | custom-call | flops 1 | bytes 1 | tf_op jit(solution)/shard_map/late/pallas_call | solution.py:208
  74.0 2.2 collective-permute-start.7
  76.2 52.3 %collective-permute-done.3.refs_3_ = f32[1024,128]{1,0:T(8,128)S(1)} collective-permute-done((f32[1024,128]{1,0:T(8,128)}, f32[1024,128]{1,0:T(8,128)S(1)}, u32[]{:S(2)}, u32[]{:S(2)}) %collective-permute-start.3) | collective-permute-done | bytes 524320 | tf_op jit(solution)/shard_map/ppermute | solution.py:285
  128.5 0.8 copy-done.3
  129.3 0.8 collective-permute-start.6
  130.1 21.9 %collective-permute-done.2.refs_2_ = f32[1024,128]{1,0:T(8,128)S(1)} collective-permute-done((f32[1024,128]{1,0:T(8,128)}, f32[1024,128]{1,0:T(8,128)S(1)}, u32[]{:S(2)}, u32[]{:S(2)}) %collective-permute-start.2) | collective-permute-done | bytes 524320 | tf_op jit(solution)/shard_map/ppermute | solution.py:285
  151.9 0.8 copy-done.5
  152.8 21.2 %collective-permute-done.1.refs_1_ = f32[1024,128]{1,0:T(8,128)S(1)} collective-permute-done((f32[1024,128]{1,0:T(8,128)}, f32[1024,128]{1,0:T(8,128)S(1)}, u32[]{:S(2)}, u32[]{:S(2)}) %collective-permute-start.1) | collective-permute-done | bytes 524320 | tf_op jit(solution)/shard_map/ppermute | solution.py:285
  173.9 0.8 copy-done.7
  181.0 12.2 %late.3.refs_8_ = f32[4096,128]{1,0:T(8,128)S(1)} custom-call(f32[4096,128]{1,0:T(8,128)} %bitcast.5.refs_0_, f32[4,2,128,128]{3,2,1,0:T(8,128)S(1)} %copy-done.1, f32[4,2,128,128]{3,2,1,0:T(8,128)S(1)} %copy-done.1, f32[128,128]{1,0:T(8,128)S(1)} %maximum_maximum_fusion.refs_3_.refs_6_, s32[32,256]{1,0:T(8,128)S(1)} %reshape.27.mask_ref.refs_4_), custom_call_target="tpu_custom_call" | custom-call | flops 1 | bytes 1 | tf_op jit(solution)/shard_map/late/pallas_call | solution.py:208
  193.2 1.3 copy-done.2
  194.5 3.2 %collective-permute-done.refs_0_ = f32[1088,128]{1,0:T(8,128)S(1)} collective-permute-done((f32[1088,128]{1,0:T(8,128)}, f32[1088,128]{1,0:T(8,128)S(1)}, u32[]{:S(2)}, u32[]{:S(2)}) %collective-permute-start) | collective-permute-done | bytes 557088 | tf_op jit(solution)/shard_map/ppermute | solution.py:285
  197.7 12.8 %late.4.zero_ref = f32[4096,128]{1,0:T(8,128)S(1)} custom-call(f32[1088,128]{1,0:T(8,128)S(1)} %collective-permute-done.refs_0_, f32[1024,128]{1,0:T(8,128)S(1)} %copy-done.8, f32[1024,128]{1,0:T(8,128)S(1)} %copy-done.6, f32[1024,128]{1,0:T(8,128)S(1)} %copy-done.4, f32[4,2,128,128]{3,2,1,0:T(8,128)S(1)} %copy-done.1, f32[4,2,128,128]{3,2,1,0:T(8,128)S(1)} %copy-done.1, ...), custom_call_target="tpu_custom_call" | custom-call | flops 1 | bytes 1 | tf_op jit(solution)/shard_map/late/pallas_call | solution.py:208
  210.5 2.6 %final.4.refs_0_ = f32[2,4096,128]{2,1,0:T(8,128)} custom-call(f32[4096,128]{1,0:T(8,128)S(1)} %late.4.zero_ref, f32[1024,128]{1,0:T(8,128)} %get-tuple-element.38.own_ref, f32[1024,128]{1,0:T(8,128)} %collective-permute-done.7.other_ref, f32[4]{0:T(128)S(1)} %pad_maximum_fusion.refs_9_.coef_ref), custom_call_target="tpu_custom_call" | custom-call | flops 1 | bytes 1 | tf_op jit(solution)/shard_map/final/pallas_call | solution.py:241
  213.1 7.1 %collective-permute-done.6.other_ref = f32[1024,128]{1,0:T(8,128)S(1)} collective-permute-done((f32[1024,128]{1,0:T(8,128)}, f32[1024,128]{1,0:T(8,128)S(1)}, u32[]{:S(2)}, u32[]{:S(2)}) %collective-permute-start.6) | collective-permute-done | bytes 524320 | tf_op jit(solution)/shard_map/ppermute | solution.py:285
  220.2 2.5 %final.5.refs_0_ = f32[2,4096,128]{2,1,0:T(8,128)} custom-call(f32[4096,128]{1,0:T(8,128)S(1)} %late.4.zero_ref, f32[1024,128]{1,0:T(8,128)} %get-tuple-element.37.own_ref, f32[1024,128]{1,0:T(8,128)S(1)} %collective-permute-done.6.other_ref, f32[4]{0:T(128)S(1)} %pad_maximum_fusion.refs_9_.coef_ref, ...), custom_call_target="tpu_custom_call", output_to_operand_aliasing={{}: (4, {})} | custom-call | flops 1 | bytes 1 | tf_op jit(solution)/shard_map/final/pallas_call | solution.py:241
  222.7 8.7 %collective-permute-done.5.other_ref = f32[1024,128]{1,0:T(8,128)S(1)} collective-permute-done((f32[1024,128]{1,0:T(8,128)}, f32[1024,128]{1,0:T(8,128)S(1)}, u32[]{:S(2)}, u32[]{:S(2)}) %collective-permute-start.5) | collective-permute-done | bytes 524320 | tf_op jit(solution)/shard_map/ppermute | solution.py:285
  231.4 2.5 %final.6.refs_0_ = f32[2,4096,128]{2,1,0:T(8,128)} custom-call(f32[4096,128]{1,0:T(8,128)S(1)} %late.4.zero_ref, f32[1024,128]{1,0:T(8,128)} %get-tuple-element.36.own_ref, f32[1024,128]{1,0:T(8,128)S(1)} %collective-permute-done.5.other_ref, f32[4]{0:T(128)S(1)} %pad_maximum_fusion.refs_9_.coef_ref, ...), custom_call_target="tpu_custom_call", output_to_operand_aliasing={{}: (4, {})} | custom-call | flops 1 | bytes 1 | tf_op jit(solution)/shard_map/final/pallas_call | solution.py:241
  233.9 8.5 %collective-permute-done.4.other_ref = f32[1024,128]{1,0:T(8,128)} collective-permute-done((f32[1024,128]{1,0:T(8,128)}, f32[1024,128]{1,0:T(8,128)}, u32[]{:S(2)}, u32[]{:S(2)}) %collective-permute-start.4) | collective-permute-done | bytes 524320 | tf_op jit(solution)/shard_map/ppermute | solution.py:285
  242.5 2.6 %final.7 = f32[2,4096,128]{2,1,0:T(8,128)} custom-call(f32[4096,128]{1,0:T(8,128)S(1)} %late.4.zero_ref, f32[1024,128]{1,0:T(8,128)} %get-tuple-element.35.own_ref, f32[1024,128]{1,0:T(8,128)} %collective-permute-done.4.other_ref, f32[4]{0:T(128)S(1)} %pad_maximum_fusion.refs_9_.coef_ref, f32[2,4096,128]{2,1,0:T(8,128)} %final.6.refs_0_), custom_call_target="tpu_custom_call", output_to_operand_aliasing={{}: (4, {})} | custom-call | flops 1 | bytes 1 | tf_op jit(solution)/shard_map/final/pallas_call | solution.py:241
  (31 shorter events, 2.0 us)
Async XLA Ops:
  2.0 1.0 copy-start
  7.3 0.8 copy-start.9
  51.1 11.3 %copy-start.10 = (f32[2,64,64]{2,1,0:T(8,128)S(1)}, f32[2,64,64]{2,1,0:T(8,128)}, u32[]{:S(2)}) copy-start(f32[2,64,64]{2,1,0:T(8,128)} %param.7) | copy-start | bytes 98308
  51.1 11.4 %copy-start.1 = (f32[4,2,128,128]{3,2,1,0:T(8,128)S(1)}, f32[4,2,128,128]{3,2,1,0:T(8,128)}, u32[]{:S(2)}) copy-start(f32[4,2,128,128]{3,2,1,0:T(8,128)} %refs_2_.3) | copy-start | bytes 1572868
  51.1 129.9 %all-to-all-start.1 = ((f32[4,1024,128]{2,1,0:T(8,128)}), f32[4,1024,128]{2,1,0:T(8,128)}, u32[]{:S(2)}, u32[]{:S(2)}) async-start(f32[4,1024,128]{2,1,0:T(8,128)} %get-tuple-element.34), calls=%async_computation.1 | async-start | bytes 4194304 | tf_op jit(solution)/shard_map/all_to_all | solution.py:288
  55.7 119.3 %copy-start.11 = (f32[3]{0:T(128)S(1)}, f32[3]{0:T(128)}, u32[]{:S(2)}) copy-start(f32[3]{0:T(128)} %param.9) | copy-start | bytes 40
  55.7 72.8 %collective-permute-start.3 = (f32[1024,128]{1,0:T(8,128)}, f32[1024,128]{1,0:T(8,128)S(1)}, u32[]{:S(2)}, u32[]{:S(2)}) collective-permute-start(f32[1024,128]{1,0:T(8,128)} %get-tuple-element.31), channel_id=1, source_target_pairs={{0,28},{1,29},{2,30},{3,31},{4,24},{5,25},{6,26},{7,27},{8,20},{9,... | collective-permute-start | bytes 1572872 | tf_op jit(solution)/shard_map/ppermute | solution.py:285
  59.4 92.5 %collective-permute-start.2 = (f32[1024,128]{1,0:T(8,128)}, f32[1024,128]{1,0:T(8,128)S(1)}, u32[]{:S(2)}, u32[]{:S(2)}) collective-permute-start(f32[1024,128]{1,0:T(8,128)} %get-tuple-element.28), channel_id=1, source_target_pairs={{0,20},{1,21},{2,22},{3,23},{4,16},{5,17},{6,18},{7,19},{8,28},{9,... | collective-permute-start | bytes 1572872 | tf_op jit(solution)/shard_map/ppermute | solution.py:285
  59.7 114.2 %collective-permute-start.1 = (f32[1024,128]{1,0:T(8,128)}, f32[1024,128]{1,0:T(8,128)S(1)}, u32[]{:S(2)}, u32[]{:S(2)}) collective-permute-start(f32[1024,128]{1,0:T(8,128)} %get-tuple-element.25), channel_id=1, source_target_pairs={{0,12},{1,13},{2,14},{3,15},{4,8},{5,9},{6,10},{7,11},{8,4},{9,5},... | collective-permute-start | bytes 1572872 | tf_op jit(solution)/shard_map/ppermute | solution.py:285
  61.6 136.1 %collective-permute-start = (f32[1088,128]{1,0:T(8,128)}, f32[1088,128]{1,0:T(8,128)S(1)}, u32[]{:S(2)}, u32[]{:S(2)}) collective-permute-start(f32[1088,128]{1,0:T(8,128)} %copy-done.9), channel_id=1, source_target_pairs={{0,4},{1,5},{2,6},{3,7},{4,0},{5,1},{6,2},{7,3},{8,12},{9,13},{10,... | collective-permute-start | bytes 1671176 | tf_op jit(solution)/shard_map/ppermute | solution.py:285
  74.0 136.6 %collective-permute-start.7 = (f32[1024,128]{1,0:T(8,128)}, f32[1024,128]{1,0:T(8,128)}, u32[]{:S(2)}, u32[]{:S(2)}) collective-permute-start(f32[1024,128]{1,0:T(8,128)} %get-tuple-element.38.own_ref), channel_id=1, source_target_pairs={{0,4},{1,5},{2,6},{3,7},{4,0},{5,1},{6,2},{7,3},{8,12},{9,13},{10,... | collective-permute-start | bytes 1572872 | tf_op jit(solution)/shard_map/ppermute | solution.py:285
  128.5 0.8 copy-start.3
  129.3 90.9 %collective-permute-start.6 = (f32[1024,128]{1,0:T(8,128)}, f32[1024,128]{1,0:T(8,128)S(1)}, u32[]{:S(2)}, u32[]{:S(2)}) collective-permute-start(f32[1024,128]{1,0:T(8,128)} %get-tuple-element.37.own_ref), channel_id=1, source_target_pairs={{0,4},{1,5},{2,6},{3,7},{4,0},{5,1},{6,2},{7,3},{8,12},{9,13},{10,... | collective-permute-start | bytes 1572872 | tf_op jit(solution)/shard_map/ppermute | solution.py:285
  151.9 0.8 copy-start.5
  152.8 78.7 %collective-permute-start.5 = (f32[1024,128]{1,0:T(8,128)}, f32[1024,128]{1,0:T(8,128)S(1)}, u32[]{:S(2)}, u32[]{:S(2)}) collective-permute-start(f32[1024,128]{1,0:T(8,128)} %get-tuple-element.36.own_ref), channel_id=1, source_target_pairs={{0,4},{1,5},{2,6},{3,7},{4,0},{5,1},{6,2},{7,3},{8,12},{9,13},{10,... | collective-permute-start | bytes 1572872 | tf_op jit(solution)/shard_map/ppermute | solution.py:285
  173.9 0.8 copy-start.7
  174.7 67.8 %collective-permute-start.4 = (f32[1024,128]{1,0:T(8,128)}, f32[1024,128]{1,0:T(8,128)}, u32[]{:S(2)}, u32[]{:S(2)}) collective-permute-start(f32[1024,128]{1,0:T(8,128)} %get-tuple-element.35.own_ref), channel_id=1, source_target_pairs={{0,4},{1,5},{2,6},{3,7},{4,0},{5,1},{6,2},{7,3},{8,12},{9,13},{10,... | collective-permute-start | bytes 1572872 | tf_op jit(solution)/shard_map/ppermute | solution.py:285
  181.0 16.8 %copy-start.4 = (f32[1024,128]{1,0:T(8,128)S(1)}, f32[1024,128]{1,0:T(8,128)}, u32[]{:S(2)}) copy-start(f32[1024,128]{1,0:T(8,128)} %copy-done.3) | copy-start | bytes 1572868
  181.0 16.8 %copy-start.6 = (f32[1024,128]{1,0:T(8,128)S(1)}, f32[1024,128]{1,0:T(8,128)}, u32[]{:S(2)}) copy-start(f32[1024,128]{1,0:T(8,128)} %copy-done.5) | copy-start | bytes 1572868
  181.0 16.8 %copy-start.8 = (f32[1024,128]{1,0:T(8,128)S(1)}, f32[1024,128]{1,0:T(8,128)}, u32[]{:S(2)}) copy-start(f32[1024,128]{1,0:T(8,128)} %copy-done.7) | copy-start | bytes 1572868
  193.2 1.3 copy-start.2
where the time goes:
time: 246 us; the launch traced here: 245 us
  waiting for transfers between devices  123 us (50%)
  Pallas kernels  64.1 us (26%)
  blocking collectives  29.7 us (12%)
  starting transfers between devices  14.5 us (6%)
  local copies, waits for them, and re-layouts  6.85 us (3%)
  between operations  5.29 us (2%)
    ppermute x8, waiting for transfers between devices, partner(): return lax.ppermute(value, ('high', 'mid'), pairs)  123 us
    pallas_call x3, Pallas kernels, late(): pl.pallas_call(functools.partial(late_kernel, half, parts, outs), grid=(1...  36.5 us
    all_to_all x1, blocking collectives, trade(): lax.all_to_all(value, 'high', split_axis=0, concat_axis=0, tiled=True)  29.7 us
    pallas_call x4, Pallas kernels, early(): pl.pallas_call(functools.partial(early_kernel, blocks // steps, tail), gr...  17.5 us
    pallas_call x4, Pallas kernels, final(): pl.pallas_call(final_kernel, grid=(steps,), in_specs=[pl.BlockSpec((size,...  10.1 us
    ppermute x8, starting transfers between devices, partner(): return lax.ppermute(value, ('high', 'mid'), pairs)  9.93 us
    unnamed x25, local copies, waits for them, and re-layouts  6.12 us
  transfers between devices with their start and end apart: 9, of which 7 were waited for; matrix products, arithmetic and copies ran while one was open for 0% of the time, Pallas kernels for 18%

commit v1 on v0

--- a/solution.py
+++ b/solution.py
@@ -9,7 +9,7 @@
 
 LANES = 128
 HALF = 64
-VMEM_LIMIT = 48 * 1024 * 1024
+VMEM_LIMIT = 60 * 1024 * 1024
 COST = pl.CostEstimate(flops=1, bytes_accessed=1, transcendentals=0)
 
 
@@ -63,7 +63,7 @@
 
 
 def early_kernel(blocks, tail, who_ref, x_ref, gate_a_ref, gate_b_ref, mask_ref, *refs):
-    part_ref, zero_ref, one_ref, wide_high, wide_low, left = refs[-6:]
+    part_ref, pair_ref, wide_high, wide_low, left = refs[-5:]
     step = pl.program_id(0)
     rows = blocks * LANES
 
@@ -78,27 +78,22 @@
         wide_high[...], wide_low[...] = split_two(jnp.concatenate(pieces, axis=0))
         left[...] = left_operand(gate_b_ref)
         if tail:
-            mask = mask_ref[...].astype(jnp.float32)
-            begin = part_ref.shape[0] - tail
-            part_ref[pl.ds(begin, tail // 2)] = mask[:, :LANES]
-            part_ref[pl.ds(begin + tail // 2, tail // 2)] = mask[:, LANES:]
+            part_ref[pl.ds(part_ref.shape[0] - tail, tail)] = mask_ref[...].astype(jnp.float32)
 
     value = jnp.concatenate([x_ref[part, 0].reshape(rows, LANES) for part in range(2)], axis=1)
     value = right_gate(value, wide_high[...], wide_low[...])
     for block in range(blocks):
         zero, one = left_gate(left[...], value[block * LANES : (block + 1) * LANES])
         part_ref[pl.ds(pl.multiple_of(step * rows, rows) + block * LANES, LANES)] = zero
-        zero_ref[0, pl.ds(block * LANES, LANES)] = zero
-        one_ref[0, pl.ds(block * LANES, LANES)] = one
-
-
-def early(who, x, gates, mask, apart, carried):
+        pair_ref[0, pl.ds(block * LANES, LANES)] = zero
+        pair_ref[1, pl.ds(block * LANES, LANES)] = one
+
+
+def early(who, x, gates, mask, apart):
     groups, blocks = x.shape[1], x.shape[2]
     rows = blocks * LANES
     steps = 2 if blocks % 2 == 0 else 1
-    tail = 2 * mask.shape[0] if apart == 0 else 0
-    full = jax.ShapeDtypeStruct((groups, rows, LANES), jnp.float32)
-    full_spec = pl.BlockSpec((1, rows // steps, LANES), lambda g, who: (who[0] ^ apart, g, 0))
+    tail = mask.shape[0] if apart == 0 else 0
     return pl.pallas_call(
         functools.partial(early_kernel, blocks // steps, tail),
         grid_spec=pltpu.PrefetchScalarGridSpec(
@@ -109,35 +104,40 @@
                 pl.BlockSpec((1, 2, LANES, LANES), lambda g, who: (0, 0, 0, 0)),
                 pl.BlockSpec((1, 2, LANES, LANES), lambda g, who: (1, 0, 0, 0)),
                 pl.BlockSpec(mask.shape, lambda g, who: (0, 0)),
-            ]
-            + [pl.BlockSpec(memory_space=pl.ANY)] * len(carried),
-            out_specs=[pl.BlockSpec((rows + tail, LANES), lambda g, who: (0, 0)), full_spec, full_spec],
+            ],
+            out_specs=[
+                pl.BlockSpec((rows + tail, LANES), lambda g, who: (0, 0)),
+                pl.BlockSpec((2, rows // steps, LANES), lambda g, who: (0, g, 0)),
+            ],
             scratch_shapes=[
                 pltpu.VMEM((2 * LANES, 2 * LANES), jnp.bfloat16),
                 pltpu.VMEM((2 * LANES, 2 * LANES), jnp.bfloat16),
                 pltpu.VMEM((4 * LANES, 2 * LANES), jnp.bfloat16),
             ],
         ),
-        out_shape=[jax.ShapeDtypeStruct((rows + tail, LANES), jnp.float32), full, full],
-        input_output_aliases={5: 1, 6: 2} if carried else {},
+        out_shape=[
+            jax.ShapeDtypeStruct((rows + tail, LANES), jnp.float32),
+            jax.ShapeDtypeStruct((2, rows, LANES), jnp.float32),
+        ],
         compiler_params=pltpu.CompilerParams(vmem_limit_bytes=VMEM_LIMIT),
         cost_estimate=COST,
         name="early",
-    )(who, x, gates, gates, mask, *carried)
+    )(who, x, gates, gates, mask)
 
 
 def mix(coef_ref, at, value):
     return coef_ref[at] * value + coef_ref[at + 1] * times_i(value)
 
 
-def late_kernel(half, parts, outs, *refs):
+def late_kernel(half, parts, outs, mixed, *refs):
     sources = refs[:parts]
-    gate_a_ref, gate_b_ref, ctrl_ref = refs[parts : parts + 3]
+    gate_a_ref, gate_b_ref, ctrl_ref, who_ref = refs[parts : parts + 4]
     held, control, left_a, left_b, right = refs[-5:]
     targets = refs[-5 - outs : -5]
-    extra = refs[parts + 3 : -5 - outs]
+    extra = refs[parts + 4 : -5 - outs]
     total = held.shape[0]
     stride = total // LANES
+    rows = total // parts
 
     left_a[...] = left_operand(gate_a_ref)
     left_b[...] = left_operand(gate_b_ref)
@@ -145,17 +145,14 @@
     right[...] = jnp.concatenate(
         [jnp.concatenate([high, high], axis=1), jnp.concatenate([low, jnp.zeros_like(low)], axis=1)], axis=0
     )
-    if parts == 1:
+    if mixed:
+        own_ref, coef_ref = extra
+        control[...] = sources[0][pl.ds(rows, control.shape[0]), :]
+    else:
         control[...] = extra[0][...].astype(jnp.float32)
-        held[...] = sources[0][...]
-    else:
-        who_ref, own_ref, coef_ref = extra
-        rows = total // parts
-        tail = control.shape[0]
-        control[:, :LANES] = sources[0][pl.ds(rows, tail), :]
-        control[:, LANES:] = sources[0][pl.ds(rows + tail, tail), :]
-        for apart in range(parts):
-            held[pl.ds(pl.multiple_of((who_ref[0] ^ apart) * rows, rows), rows), :] = sources[apart][pl.ds(0, rows), :]
+    for apart in range(parts):
+        place = pl.multiple_of((who_ref[0] ^ apart) * rows, rows)
+        held[pl.ds(place, rows), :] = sources[apart][pl.ds(0, rows), :] if mixed else sources[apart][0]
 
     @pl.loop(0, stride // 4)
     def _(step):
@@ -184,7 +181,8 @@
             acted = acted[:, :LANES] + acted[:, LANES:]
             chosen = []
             for block in range(blocks):
-                row = control[pl.ds(out * (span // LANES) + step * blocks + block, 1), :]
+                at = (out * (span // LANES) + step * blocks + block) * 2
+                row = jnp.concatenate([control[pl.ds(at, 1), :], control[pl.ds(at + 1, 1), :]], axis=1)
                 chosen.append(jnp.where(picked, jnp.broadcast_to(row, picked.shape), 0.0))
             chosen = matmul(jnp.concatenate(chosen, axis=0).astype(jnp.bfloat16), ones)
             value = jnp.where(chosen > 0.5, acted, value)
@@ -194,26 +192,28 @@
                 )
                 for side, piece in enumerate(left_gate(left_b[...], both)):
                     place = pl.ds(begin + (block + side) * LANES, LANES)
-                    if parts > 1:
+                    if mixed:
                         piece = mix(coef_ref, 0, own_ref[place, :]) + mix(coef_ref, 2, piece)
                     target[place, :] = piece
 
 
-def late(sources, gates, ctrl, half, outs, *extra):
+def late(sources, gates, ctrl, who, half, outs, *extra):
     parts = len(sources)
-    total = sources[-1].shape[0] * parts
+    rows = sources[-1].shape[-2]
+    total = rows * parts
     vmem = pl.BlockSpec(memory_space=pltpu.VMEM)
     smem = pl.BlockSpec(memory_space=pltpu.SMEM)
+    source = vmem if len(extra) == 2 else pl.BlockSpec((1, rows, LANES), lambda g: (half, 0, 0))
     gate_specs = [pl.BlockSpec((1, 2, LANES, LANES), lambda g, at=at: (at, 0, 0, 0)) for at in (2, 3)]
     return pl.pallas_call(
-        functools.partial(late_kernel, half, parts, outs),
+        functools.partial(late_kernel, half, parts, outs, len(extra) == 2),
         grid=(1,),
-        in_specs=[vmem] * parts + gate_specs + [vmem] + ([vmem] if parts == 1 else [smem, vmem, smem]),
+        in_specs=[source] * parts + gate_specs + [vmem, smem] + ([vmem, smem] if len(extra) == 2 else [vmem]),
         out_specs=[vmem] * outs,
         out_shape=[jax.ShapeDtypeStruct((total // outs, LANES), jnp.float32)] * outs,
         scratch_shapes=[
             pltpu.VMEM((total, LANES), jnp.float32),
-            pltpu.VMEM((total // LANES, 2 * LANES), jnp.float32),
+            pltpu.VMEM((total // HALF, LANES), jnp.float32),
             pltpu.VMEM((4 * LANES, 2 * LANES), jnp.bfloat16),
             pltpu.VMEM((4 * LANES, 2 * LANES), jnp.bfloat16),
             pltpu.VMEM((2 * LANES, 2 * LANES), jnp.bfloat16),
@@ -221,7 +221,7 @@
         compiler_params=pltpu.CompilerParams(vmem_limit_bytes=VMEM_LIMIT),
         cost_estimate=COST,
         name="late",
-    )(*sources, gates, gates, ctrl, *extra)
+    )(*sources, gates, gates, ctrl, who, *extra)
 
 
 def final_kernel(zero_ref, own_ref, other_ref, coef_ref, *refs):
@@ -265,6 +265,10 @@
     )
 
 
+def after(value, *others):
+    return lax.optimization_barrier((value, *others))[0]
+
+
 def wide_ctrl(ctrl_gate):
     return jnp.block([[ctrl_gate[0], -ctrl_gate[1]], [ctrl_gate[1], ctrl_gate[0]]])
 
@@ -278,31 +282,32 @@
     parity = lax.axis_index("mid") >> top_bit & 1
     who = lax.axis_index("high").astype(jnp.int32).reshape(1)
 
-    def partner(value, apart=0):
+    def move(value, apart, across=1):
         pairs = [
-            (high * mid + at, (high ^ apart) * mid + (at ^ 1 << top_bit)) for high in range(groups) for at in range(mid)
+            (high * mid + at, (high ^ apart) * mid + (at ^ across << top_bit))
+            for high in range(groups)
+            for at in range(mid)
         ]
         return lax.ppermute(value, ("high", "mid"), pairs)
 
-    def trade(value):
-        return lax.all_to_all(value, "high", split_axis=0, concat_axis=0, tiled=True).reshape(total, LANES)
-
     x = amplitudes.reshape(2, groups, total // groups // LANES, LANES, LANES)
-    mask = control_mask.reshape(total // LANES, 2 * LANES)
-    carried, away = (), []
+    mask = control_mask.reshape(total // HALF, LANES)
+    away, pairs = [], []
     for apart in range(groups):
-        part, *carried = early(who, x, layer_gates, mask, apart, carried)
-        away.append(partner(part, apart))
-    zero, one = carried
+        part, pair = early(who, x, layer_gates, mask, apart)
+        away.append(move(part, apart))
+        pairs.append(pair)
+    for apart in range(1, groups):
+        pair = after(pairs[apart], away[0]) if apart == 1 else pairs[apart]
+        pairs[apart] = move(pair, apart, 0)
     ctrl = wide_ctrl(ctrl_gate)
     coefs = coefficients(mid_angles, parity)
     outs = 4
-    one = trade(one)
-    own_one = late([one], layer_gates, ctrl, 1, outs, mask)
-    other_one = [partner(piece) for piece in own_one]
-    zero, _ = lax.optimization_barrier((zero, one))
-    (own_zero,) = late([trade(zero)], layer_gates, ctrl, 0, 1, mask)
-    (mixed,) = late(away, layer_gates, ctrl, 0, 1, who, own_zero, coefs)
+    pairs[0] = after(pairs[0], *away[1:3])
+    own_one = late(pairs, layer_gates, ctrl, who, 1, outs, mask)
+    other_one = [move(piece, 0) for piece in own_one]
+    (own_zero,) = late(pairs, layer_gates, ctrl, who, 0, 1, mask)
+    (mixed,) = late(away, layer_gates, ctrl, who, 0, 1, own_zero, coefs)
     result = ()
     for at in range(outs):
         result = (final(mixed, own_one[at], other_one[at], coefs, at, result),)

time: 246 us -> 207 us (0.84)
  blocking collectives: 29.7 us -> 0 us
  waiting for transfers between devices: 123 us -> 107 us
  Pallas kernels: 64.1 us -> 70.2 us
    all_to_all x1 -> x0, blocking collectives: 29.7 us -> none  [trade(): lax.all_to_all(value, 'high', split_axis=0, concat_axis=0, tiled=True)]
    ppermute x8 -> x11, waiting for transfers between devices: 123 us -> 107 us  [move(): return lax.ppermute(value, ('high', 'mid'), pairs)]
    ppermute x8 -> x11, starting transfers between devices: 9.93 us -> 15.8 us  [move(): return lax.ppermute(value, ('high', 'mid'), pairs)]
    pallas_call x3, Pallas kernels: 36.5 us -> 41.1 us  [late(): pl.pallas_call(functools.partial(late_kernel, half, parts, outs, len(extr...]
    all_to_all x1 -> x0, starting transfers between devices: 4.6 us -> none  [trade(): lax.all_to_all(value, 'high', split_axis=0, concat_axis=0, tiled=True)]
    unnamed x25 -> x24, local copies, waits for them, and re-layouts: 6.12 us -> 5.93 us
  transfers between devices with their start and end apart: 9 -> 11, of which waited for: 7 -> 7; matrix products, arithmetic and copies ran while one was open for 0% -> 1% of each run, Pallas kernels for 18% -> 31%
where the time goes in v1:
time: 207 us; the launch traced here: 206 us
  waiting for transfers between devices  107 us (52%)
  Pallas kernels  70.2 us (34%)
  starting transfers between devices  15.8 us (8%)
  local copies, waits for them, and re-layouts  6.64 us (3%)
  between operations  5.02 us (2%)
    ppermute x11, waiting for transfers between devices, move(): return lax.ppermute(value, ('high', 'mid'), pairs)  107 us
    pallas_call x3, Pallas kernels, late(): pl.pallas_call(functools.partial(late_kernel, half, parts, outs, len(extr...  41.1 us
    pallas_call x4, Pallas kernels, early(): pl.pallas_call(functools.partial(early_kernel, blocks // steps, tail), gr...  18.4 us
    ppermute x11, starting transfers between devices, move(): return lax.ppermute(value, ('high', 'mid'), pairs)  15.8 us
    pallas_call x4, Pallas kernels, final(): pl.pallas_call(final_kernel, grid=(steps,), in_specs=[pl.BlockSpec((size,...  10.6 us
    unnamed x24, local copies, waits for them, and re-layouts  5.93 us
  transfers between devices with their start and end apart: 11, of which 7 were waited for; matrix products, arithmetic and copies ran while one was open for 1% of the time, Pallas kernels for 31%

profile of v1, /device:TPU:0, one launch (start us, length us, event | category | flops | bytes accessed | tf_op | source)
XLA Modules:
  0.0 206.1 jit_solution(18274880194816970843)
XLA Ops:
  0.0 4.6 %early.4 = (f32[1088,128]{1,0:T(8,128)}, f32[2,1024,128]{2,1,0:T(8,128)}) custom-call(s32[1]{0:T(128)} %bitcast.who_ref.refs_7_, f32[2,4,8,128,128]{4,3,2,1,0:T(8,128)} %bitcast.14, f32[4,2,128,128]{3,2,1,0:T(8,128)} %refs_5_.5, f32[4,2,128,128]{3,2,1,0:T(8,128)} %refs_5_.5, s32[64,128]{1,0:T(8,128)} %bitcast.18), custom_call_target="tpu_custom_call" | custom-call | flops 1 | bytes 1 | tf_op jit(solution)/shard_map/early/pallas_call | solution.py:97
  4.6 4.0 %collective-permute-start = (f32[1088,128]{1,0:T(8,128)}, f32[1088,128]{1,0:T(8,128)S(1)}, u32[]{:S(2)}, u32[]{:S(2)}) collective-permute-start(f32[1088,128]{1,0:T(8,128)} %get-tuple-element.19), channel_id=1, source_target_pairs={{0,4},{1,5},{2,6},{3,7},{4,0},{5,1},{6,2},{7,3},{8,12},{9,13},{10,... | collective-permute-start | bytes 1671176 | tf_op jit(solution)/shard_map/ppermute | solution.py:291
  8.7 4.6 %early.6 = (f32[1024,128]{1,0:T(8,128)}, f32[2,1024,128]{2,1,0:T(8,128)}) custom-call(s32[1]{0:T(128)} %bitcast.who_ref.refs_7_, f32[2,4,8,128,128]{4,3,2,1,0:T(8,128)} %bitcast.15, f32[4,2,128,128]{3,2,1,0:T(8,128)} %refs_5_.5, f32[4,2,128,128]{3,2,1,0:T(8,128)} %refs_5_.5, s32[64,128]{1,0:T(8,128)} %bitcast.19), custom_call_target="tpu_custom_call" | custom-call | flops 1 | bytes 1 | tf_op jit(solution)/shard_map/early/pallas_call | solution.py:97
  13.2 1.5 collective-permute-start.5
  14.8 4.6 %early.7 = (f32[1024,128]{1,0:T(8,128)}, f32[2,1024,128]{2,1,0:T(8,128)}) custom-call(s32[1]{0:T(128)} %bitcast.who_ref.refs_7_, f32[2,4,8,128,128]{4,3,2,1,0:T(8,128)} %bitcast.16, f32[4,2,128,128]{3,2,1,0:T(8,128)} %refs_5_.5, f32[4,2,128,128]{3,2,1,0:T(8,128)} %refs_5_.5, s32[64,128]{1,0:T(8,128)} %bitcast.20), custom_call_target="tpu_custom_call" | custom-call | flops 1 | bytes 1 | tf_op jit(solution)/shard_map/early/pallas_call | solution.py:97
  19.4 4.6 %early.5 = (f32[1024,128]{1,0:T(8,128)}, f32[2,1024,128]{2,1,0:T(8,128)}) custom-call(s32[1]{0:T(128)} %bitcast.who_ref.refs_7_, f32[2,4,8,128,128]{4,3,2,1,0:T(8,128)} %bitcast.17, f32[4,2,128,128]{3,2,1,0:T(8,128)} %refs_5_.5, f32[4,2,128,128]{3,2,1,0:T(8,128)} %refs_5_.5, s32[64,128]{1,0:T(8,128)} %bitcast.21), custom_call_target="tpu_custom_call" | custom-call | flops 1 | bytes 1 | tf_op jit(solution)/shard_map/early/pallas_call | solution.py:97
  24.0 9.4 %collective-permute-done.refs_0_ = f32[1088,128]{1,0:T(8,128)S(1)} collective-permute-done((f32[1088,128]{1,0:T(8,128)}, f32[1088,128]{1,0:T(8,128)S(1)}, u32[]{:S(2)}, u32[]{:S(2)}) %collective-permute-start) | collective-permute-done | bytes 557088 | tf_op jit(solution)/shard_map/ppermute | solution.py:291
  33.4 4.0 %collective-permute-start.2 = (f32[1024,128]{1,0:T(8,128)}, f32[1024,128]{1,0:T(8,128)S(1)}, u32[]{:S(2)}, u32[]{:S(2)}) collective-permute-start(f32[1024,128]{1,0:T(8,128)} %get-tuple-element.21), channel_id=1, source_target_pairs={{0,20},{1,21},{2,22},{3,23},{4,16},{5,17},{6,18},{7,19},{8,28},{9,... | collective-permute-start | bytes 1572872 | tf_op jit(solution)/shard_map/ppermute | solution.py:291
  37.5 0.7 maximum_maximum_fusion.refs_6_
  38.2 32.4 %collective-permute-done.1.refs_1_ = f32[1024,128]{1,0:T(8,128)S(1)} collective-permute-done((f32[1024,128]{1,0:T(8,128)}, f32[1024,128]{1,0:T(8,128)S(1)}, u32[]{:S(2)}, u32[]{:S(2)}) %collective-permute-start.1) | collective-permute-done | bytes 524320 | tf_op jit(solution)/shard_map/ppermute | solution.py:291
  71.0 24.4 %collective-permute-done.2.refs_2_ = f32[1024,128]{1,0:T(8,128)S(1)} collective-permute-done((f32[1024,128]{1,0:T(8,128)}, f32[1024,128]{1,0:T(8,128)S(1)}, u32[]{:S(2)}, u32[]{:S(2)}) %collective-permute-start.2) | collective-permute-done | bytes 524320 | tf_op jit(solution)/shard_map/ppermute | solution.py:291
  95.4 0.8 copy-done.5
  96.5 0.6 copy-done.1
  97.1 1.0 copy-done.2
  98.1 12.9 %late.5 = (f32[1024,128]{1,0:T(8,128)}, f32[1024,128]{1,0:T(8,128)}, f32[1024,128]{1,0:T(8,128)}, f32[1024,128]{1,0:T(8,128)}) custom-call(f32[2,1024,128]{2,1,0:T(8,128)} %get-tuple-element.24.refs_0_, f32[2,1024,128]{2,1,0:T(8,128)} %copy-done.2, f32[2,1024,128]{2,1,0:T(8,128)} %copy-done, f32[2,1024,128]{2,1,0:T(8,128)} %copy-done.1, ...), custom_call_target="tpu_custom_call" | custom-call | flops 1 | bytes 1 | tf_op jit(solution)/shard_map/late/pallas_call | solution.py:208
  111.0 2.9 %collective-permute-start.9 = (f32[1024,128]{1,0:T(8,128)}, f32[1024,128]{1,0:T(8,128)S(1)}, u32[]{:S(2)}, u32[]{:S(2)}) collective-permute-start(f32[1024,128]{1,0:T(8,128)} %get-tuple-element.31.own_ref), channel_id=1, source_target_pairs={{0,4},{1,5},{2,6},{3,7},{4,0},{5,1},{6,2},{7,3},{8,12},{9,13},{10,... | collective-permute-start | bytes 1572872 | tf_op jit(solution)/shard_map/ppermute | solution.py:291
  114.0 2.9 %collective-permute-start.7 = (f32[1024,128]{1,0:T(8,128)}, f32[1024,128]{1,0:T(8,128)S(1)}, u32[]{:S(2)}, u32[]{:S(2)}) collective-permute-start(f32[1024,128]{1,0:T(8,128)} %get-tuple-element.29.own_ref), channel_id=1, source_target_pairs={{0,4},{1,5},{2,6},{3,7},{4,0},{5,1},{6,2},{7,3},{8,12},{9,13},{10,... | collective-permute-start | bytes 1572872 | tf_op jit(solution)/shard_map/ppermute | solution.py:291
  116.9 0.7 fusion.1
  123.1 13.4 %late.3.refs_8_ = f32[4096,128]{1,0:T(8,128)} custom-call(f32[2,1024,128]{2,1,0:T(8,128)} %get-tuple-element.24.refs_0_, f32[2,1024,128]{2,1,0:T(8,128)} %copy-done.2, f32[2,1024,128]{2,1,0:T(8,128)} %copy-done, f32[2,1024,128]{2,1,0:T(8,128)} %copy-done.1, f32[4,2,128,128]{3,2,1,0:T(8,128)} %refs_5_.5, f32[4,2,128,128]{3,2,1,0:T(8,128)} %refs_5_.5, ...), custom_call_target="tpu_custom_call" | custom-call | flops 1 | bytes 1 | tf_op jit(solution)/shard_map/late/pallas_call | solution.py:208
  136.5 14.9 %late.4.zero_ref = f32[4096,128]{1,0:T(8,128)} custom-call(f32[1088,128]{1,0:T(8,128)} %copy-done.3, f32[1024,128]{1,0:T(8,128)} %copy-done.4, f32[1024,128]{1,0:T(8,128)} %copy-done.5, f32[1024,128]{1,0:T(8,128)} %collective-permute-done.3.refs_3_, f32[4,2,128,128]{3,2,1,0:T(8,128)} %refs_5_.5, f32[4,2,128,128]{3,2,1,0:T(8,128)} %refs_5_.5, ...), custom_call_target="tpu_custom_call" | custom-call | flops 1 | bytes 1 | tf_op jit(solution)/shard_map/late/pallas_call | solution.py:208
  151.4 17.6 %collective-permute-done.10.other_ref = f32[1024,128]{1,0:T(8,128)S(1)} collective-permute-done((f32[1024,128]{1,0:T(8,128)}, f32[1024,128]{1,0:T(8,128)S(1)}, u32[]{:S(2)}, u32[]{:S(2)}) %collective-permute-start.10) | collective-permute-done | bytes 524320 | tf_op jit(solution)/shard_map/ppermute | solution.py:291
  169.0 0.8 copy-done.9
  169.8 2.6 %final.4.refs_0_ = f32[2,4096,128]{2,1,0:T(8,128)} custom-call(f32[4096,128]{1,0:T(8,128)} %late.4.zero_ref, f32[1024,128]{1,0:T(8,128)} %get-tuple-element.32.own_ref, f32[1024,128]{1,0:T(8,128)} %copy-done.9, f32[4]{0:T(128)} %pad_maximum_fusion.refs_9_.coef_ref), custom_call_target="tpu_custom_call" | custom-call | flops 1 | bytes 1 | tf_op jit(solution)/shard_map/final/pallas_call | solution.py:241
  172.4 7.8 %collective-permute-done.9.other_ref = f32[1024,128]{1,0:T(8,128)S(1)} collective-permute-done((f32[1024,128]{1,0:T(8,128)}, f32[1024,128]{1,0:T(8,128)S(1)}, u32[]{:S(2)}, u32[]{:S(2)}) %collective-permute-start.9) | collective-permute-done | bytes 524320 | tf_op jit(solution)/shard_map/ppermute | solution.py:291
  180.2 0.8 copy-done.8
  181.0 2.7 %final.5.refs_0_ = f32[2,4096,128]{2,1,0:T(8,128)} custom-call(f32[4096,128]{1,0:T(8,128)} %late.4.zero_ref, f32[1024,128]{1,0:T(8,128)} %get-tuple-element.31.own_ref, f32[1024,128]{1,0:T(8,128)} %copy-done.8, f32[4]{0:T(128)} %pad_maximum_fusion.refs_9_.coef_ref, f32[2,4096,128]{2,1,0:T(8,128)} %final.4.refs_0_), custom_call_target="tpu_custom_call", output_to_operand_aliasing={{}: (4, {})} | custom-call | flops 1 | bytes 1 | tf_op jit(solution)/shard_map/final/pallas_call | solution.py:241
  183.7 7.8 %collective-permute-done.8.other_ref = f32[1024,128]{1,0:T(8,128)S(1)} collective-permute-done((f32[1024,128]{1,0:T(8,128)}, f32[1024,128]{1,0:T(8,128)S(1)}, u32[]{:S(2)}, u32[]{:S(2)}) %collective-permute-start.8) | collective-permute-done | bytes 524320 | tf_op jit(solution)/shard_map/ppermute | solution.py:291
  191.5 0.8 copy-done.7
  192.3 2.7 %final.6.refs_0_ = f32[2,4096,128]{2,1,0:T(8,128)} custom-call(f32[4096,128]{1,0:T(8,128)} %late.4.zero_ref, f32[1024,128]{1,0:T(8,128)} %get-tuple-element.30.own_ref, f32[1024,128]{1,0:T(8,128)} %copy-done.7, f32[4]{0:T(128)} %pad_maximum_fusion.refs_9_.coef_ref, f32[2,4096,128]{2,1,0:T(8,128)} %final.5.refs_0_), custom_call_target="tpu_custom_call", output_to_operand_aliasing={{}: (4, {})} | custom-call | flops 1 | bytes 1 | tf_op jit(solution)/shard_map/final/pallas_call | solution.py:241
  194.9 7.7 %collective-permute-done.7.other_ref = f32[1024,128]{1,0:T(8,128)S(1)} collective-permute-done((f32[1024,128]{1,0:T(8,128)}, f32[1024,128]{1,0:T(8,128)S(1)}, u32[]{:S(2)}, u32[]{:S(2)}) %collective-permute-start.7) | collective-permute-done | bytes 524320 | tf_op jit(solution)/shard_map/ppermute | solution.py:291
  202.6 0.8 copy-done.6
  203.4 2.7 %final.7 = f32[2,4096,128]{2,1,0:T(8,128)} custom-call(f32[4096,128]{1,0:T(8,128)} %late.4.zero_ref, f32[1024,128]{1,0:T(8,128)} %get-tuple-element.29.own_ref, f32[1024,128]{1,0:T(8,128)} %copy-done.6, f32[4]{0:T(128)} %pad_maximum_fusion.refs_9_.coef_ref, f32[2,4096,128]{2,1,0:T(8,128)} %final.6.refs_0_), custom_call_target="tpu_custom_call", output_to_operand_aliasing={{}: (4, {})} | custom-call | flops 1 | bytes 1 | tf_op jit(solution)/shard_map/final/pallas_call | solution.py:241
  (31 shorter events, 1.5 us)
Async XLA Ops:
  4.6 28.8 %collective-permute-start = (f32[1088,128]{1,0:T(8,128)}, f32[1088,128]{1,0:T(8,128)S(1)}, u32[]{:S(2)}, u32[]{:S(2)}) collective-permute-start(f32[1088,128]{1,0:T(8,128)} %get-tuple-element.19), channel_id=1, source_target_pairs={{0,4},{1,5},{2,6},{3,7},{4,0},{5,1},{6,2},{7,3},{8,12},{9,13},{10,... | collective-permute-start | bytes 1671176 | tf_op jit(solution)/shard_map/ppermute | solution.py:291
  13.2 24.3 %copy-start.10 = (f32[2,64,64]{2,1,0:T(8,128)S(1)}, f32[2,64,64]{2,1,0:T(8,128)}, u32[]{:S(2)}) copy-start(f32[2,64,64]{2,1,0:T(8,128)} %param.7) | copy-start | bytes 98308
  13.2 82.1 %collective-permute-start.5 = (f32[2,1024,128]{2,1,0:T(8,128)}, f32[2,1024,128]{2,1,0:T(8,128)S(1)}, u32[]{:S(2)}, u32[]{:S(2)}) collective-permute-start(f32[2,1024,128]{2,1,0:T(8,128)} %get-tuple-element.27), channel_id=1, source_target_pairs={{0,16},{1,17},{2,18},{3,19},{4,20},{5,21},{6,22},{7,23},{8,24},{9,... | collective-permute-start | bytes 3145736 | tf_op jit(solution)/shard_map/ppermute | solution.py:291
  19.4 97.4 %copy-start.11 = (f32[3]{0:T(128)S(1)}, f32[3]{0:T(128)}, u32[]{:S(2)}) copy-start(f32[3]{0:T(128)} %param.9) | copy-start | bytes 40
  19.4 76.0 %collective-permute-start.6 = (f32[2,1024,128]{2,1,0:T(8,128)}, f32[2,1024,128]{2,1,0:T(8,128)S(1)}, u32[]{:S(2)}, u32[]{:S(2)}) collective-permute-start(f32[2,1024,128]{2,1,0:T(8,128)} %get-tuple-element.28), channel_id=1, source_target_pairs={{0,24},{1,25},{2,26},{3,27},{4,28},{5,29},{6,30},{7,31},{8,16},{9,... | collective-permute-start | bytes 3145736 | tf_op jit(solution)/shard_map/ppermute | solution.py:291
  33.4 77.5 %copy-start.3 = (f32[1088,128]{1,0:T(8,128)}, f32[1088,128]{1,0:T(8,128)S(1)}, u32[]{:S(2)}) copy-start(f32[1088,128]{1,0:T(8,128)S(1)} %collective-permute-done.refs_0_) | copy-start | bytes 1671172
  33.4 62.7 %collective-permute-start.4 = (f32[2,1024,128]{2,1,0:T(8,128)}, f32[2,1024,128]{2,1,0:T(8,128)S(1)}, u32[]{:S(2)}, u32[]{:S(2)}) collective-permute-start(f32[2,1024,128]{2,1,0:T(8,128)} %get-tuple-element.26), channel_id=1, source_target_pairs={{0,8},{1,9},{2,10},{3,11},{4,12},{5,13},{6,14},{7,15},{8,0},{9,1},... | collective-permute-start | bytes 3145736 | tf_op jit(solution)/shard_map/ppermute | solution.py:291
  33.4 37.2 %collective-permute-start.1 = (f32[1024,128]{1,0:T(8,128)}, f32[1024,128]{1,0:T(8,128)S(1)}, u32[]{:S(2)}, u32[]{:S(2)}) collective-permute-start(f32[1024,128]{1,0:T(8,128)} %get-tuple-element.20), channel_id=1, source_target_pairs={{0,12},{1,13},{2,14},{3,15},{4,8},{5,9},{6,10},{7,11},{8,4},{9,5},... | collective-permute-start | bytes 1572872 | tf_op jit(solution)/shard_map/ppermute | solution.py:291
  33.4 61.9 %collective-permute-start.2 = (f32[1024,128]{1,0:T(8,128)}, f32[1024,128]{1,0:T(8,128)S(1)}, u32[]{:S(2)}, u32[]{:S(2)}) collective-permute-start(f32[1024,128]{1,0:T(8,128)} %get-tuple-element.21), channel_id=1, source_target_pairs={{0,20},{1,21},{2,22},{3,23},{4,16},{5,17},{6,18},{7,19},{8,28},{9,... | collective-permute-start | bytes 1572872 | tf_op jit(solution)/shard_map/ppermute | solution.py:291
  70.6 24.8 %copy-start.4 = (f32[1024,128]{1,0:T(8,128)}, f32[1024,128]{1,0:T(8,128)S(1)}, u32[]{:S(2)}) copy-start(f32[1024,128]{1,0:T(8,128)S(1)} %collective-permute-done.1.refs_1_) | copy-start | bytes 1572868
  70.6 65.9 %collective-permute-start.3 = (f32[1024,128]{1,0:T(8,128)}, f32[1024,128]{1,0:T(8,128)}, u32[]{:S(2)}, u32[]{:S(2)}) collective-permute-start(f32[1024,128]{1,0:T(8,128)} %get-tuple-element.22), channel_id=1, source_target_pairs={{0,28},{1,29},{2,30},{3,31},{4,24},{5,25},{6,26},{7,27},{8,20},{9,... | collective-permute-start | bytes 1572872 | tf_op jit(solution)/shard_map/ppermute | solution.py:291
  95.4 0.8 copy-start.5
  95.4 1.1 copy-start
  96.1 1.0 copy-start.1
  97.1 1.0 copy-start.2
  111.0 58.0 %collective-permute-start.10 = (f32[1024,128]{1,0:T(8,128)}, f32[1024,128]{1,0:T(8,128)S(1)}, u32[]{:S(2)}, u32[]{:S(2)}) collective-permute-start(f32[1024,128]{1,0:T(8,128)} %get-tuple-element.32.own_ref), channel_id=1, source_target_pairs={{0,4},{1,5},{2,6},{3,7},{4,0},{5,1},{6,2},{7,3},{8,12},{9,13},{10,... | collective-permute-start | bytes 1572872 | tf_op jit(solution)/shard_map/ppermute | solution.py:291
  111.0 69.3 %collective-permute-start.9 = (f32[1024,128]{1,0:T(8,128)}, f32[1024,128]{1,0:T(8,128)S(1)}, u32[]{:S(2)}, u32[]{:S(2)}) collective-permute-start(f32[1024,128]{1,0:T(8,128)} %get-tuple-element.31.own_ref), channel_id=1, source_target_pairs={{0,4},{1,5},{2,6},{3,7},{4,0},{5,1},{6,2},{7,3},{8,12},{9,13},{10,... | collective-permute-start | bytes 1572872 | tf_op jit(solution)/shard_map/ppermute | solution.py:291
  113.9 77.6 %collective-permute-start.8 = (f32[1024,128]{1,0:T(8,128)}, f32[1024,128]{1,0:T(8,128)S(1)}, u32[]{:S(2)}, u32[]{:S(2)}) collective-permute-start(f32[1024,128]{1,0:T(8,128)} %get-tuple-element.30.own_ref), channel_id=1, source_target_pairs={{0,4},{1,5},{2,6},{3,7},{4,0},{5,1},{6,2},{7,3},{8,12},{9,13},{10,... | collective-permute-start | bytes 1572872 | tf_op jit(solution)/shard_map/ppermute | solution.py:291
  114.0 88.6 %collective-permute-start.7 = (f32[1024,128]{1,0:T(8,128)}, f32[1024,128]{1,0:T(8,128)S(1)}, u32[]{:S(2)}, u32[]{:S(2)}) collective-permute-start(f32[1024,128]{1,0:T(8,128)} %get-tuple-element.29.own_ref), channel_id=1, source_target_pairs={{0,4},{1,5},{2,6},{3,7},{4,0},{5,1},{6,2},{7,3},{8,12},{9,13},{10,... | collective-permute-start | bytes 1572872 | tf_op jit(solution)/shard_map/ppermute | solution.py:291
  169.0 0.8 copy-start.9
  180.2 0.8 copy-start.8
  191.5 0.8 copy-start.7
  202.6 0.8 copy-start.6

commit v2 on v1

v2 whole, which is shorter than its diff:
```python
import functools

import jax
import jax.numpy as jnp
from jax import lax
from jax.experimental import pallas as pl
from jax.experimental.pallas import tpu as pltpu
from jax.sharding import PartitionSpec as P

LANES = 128
HALF = 64
EARLY_LIMIT = 60 * 1024 * 1024
LATE_LIMIT = 32 * 1024 * 1024
FINAL_LIMIT = 16 * 1024 * 1024
COST = pl.CostEstimate(flops=1, bytes_accessed=1, transcendentals=0)


def split_two(value):
    high = value.astype(jnp.bfloat16)
    low = (value - high.astype(jnp.float32)).astype(jnp.bfloat16)
    return high, low


def matmul(left, right):
    return lax.dot_general(left, right, (((1,), (0,)), ((), ())), preferred_element_type=jnp.float32)


def matmul_nt(left, right):
    return lax.dot_general(left, right, (((1,), (1,)), ((), ())), preferred_element_type=jnp.float32)


def right_gate(value, gate_high, gate_low):
    high, low = split_two(value)
    return matmul_nt(high, gate_high) + (matmul_nt(low, gate_high) + matmul_nt(high, gate_low))


def times_i(value):
    lane = lax.broadcasted_iota(jnp.int32, value.shape, 1)
    turned = pltpu.roll(value, HALF, 1)
    return jnp.where(lane < HALF, -turned, turned)


def left_operand(gate_ref):
    return jnp.concatenate(split_two(jnp.concatenate([gate_ref[0, 0], gate_ref[0, 1]], axis=1)), axis=0)


def left_gate(gate, value):
    turned = [times_i(value[:, begin : begin + LANES]) for begin in (0, LANES)]
    high, low = split_two(jnp.concatenate([value, jnp.concatenate(turned, axis=1)], axis=0))
    product = matmul(gate, high)
    product = product[:LANES] + (product[LANES:] + matmul(gate[:LANES], low))
    return product[:, :LANES], product[:, LANES:]


def early_kernel(tail, who_ref, x_ref, gate_a_ref, gate_b_ref, mask_ref, part_ref, pair_ref):
    rows = pair_ref.shape[1]
    if tail:
        part_ref[pl.ds(rows, tail)] = mask_ref[...].astype(jnp.float32)
    real, imag = gate_a_ref[0, 0], gate_a_ref[0, 1]
    pieces = []
    for begin in (0, HALF):
        piece_real, piece_imag = real[begin : begin + HALF], imag[begin : begin + HALF]
        pieces.append(jnp.concatenate([piece_real, -piece_imag], axis=1))
        pieces.append(jnp.concatenate([piece_imag, piece_real], axis=1))
    wide_high, wide_low = split_two(jnp.concatenate(pieces, axis=0))
    left = left_operand(gate_b_ref)
    value = jnp.concatenate([x_ref[part, 0].reshape(rows, LANES) for part in range(2)], axis=1)
    value = right_gate(value, wide_high, wide_low)
    for begin in range(0, rows, LANES):
        zero, one = left_gate(left, value[begin : begin + LANES])
        part_ref[pl.ds(begin, LANES)] = zero
        pair_ref[0, pl.ds(begin, LANES)] = zero
        pair_ref[1, pl.ds(begin, LANES)] = one


def early(who, x, gates, mask, apart, chunk, chunks):
    blocks = x.shape[2] // chunks
    rows = blocks * LANES
    tail = mask.shape[0] if apart == 0 and chunk == 0 else 0
    return pl.pallas_call(
        functools.partial(early_kernel, tail),
        grid_spec=pltpu.PrefetchScalarGridSpec(
            num_scalar_prefetch=1,
            grid=(1,),
            in_specs=[
                pl.BlockSpec((2, 1, blocks, LANES, LANES), lambda g, who: (0, who[0] ^ apart, chunk, 0, 0)),
                pl.BlockSpec((1, 2, LANES, LANES), lambda g, who: (0, 0, 0, 0)),
                pl.BlockSpec((1, 2, LANES, LANES), lambda g, who: (1, 0, 0, 0)),
                pl.BlockSpec(mask.shape, lambda g, who: (0, 0)),
            ],
            out_specs=[
                pl.BlockSpec((rows + tail, LANES), lambda g, who: (0, 0)),
                pl.BlockSpec((2, rows, LANES), lambda g, who: (0, 0, 0)),
            ],
        ),
        out_shape=[
            jax.ShapeDtypeStruct((rows + tail, LANES), jnp.float32),
            jax.ShapeDtypeStruct((2, rows, LANES), jnp.float32),
        ],
        compiler_params=pltpu.CompilerParams(vmem_limit_bytes=EARLY_LIMIT),
        cost_estimate=COST,
        name="early",
    )(who, x, gates, gates, mask)


def mix(coef_ref, at, value):
    return coef_ref[at] * value + coef_ref[at + 1] * times_i(value)


def late_kernel(half, places, sizes, mixed, *refs):
    sources = refs[: len(places)]
    gate_a_ref, gate_b_ref, ctrl_ref, who_ref = refs[len(places) : len(places) + 4]
    held, control, left_a, left_b, right = refs[-5:]
    targets = refs[-5 - len(sizes) : -5]
    extra = refs[len(places) + 4 : -5 - len(sizes)]
    total = held.shape[0]
    stride = total // LANES

    left_a[...] = left_operand(gate_a_ref)
    left_b[...] = left_operand(gate_b_ref)
    high, low = split_two(ctrl_ref[...])
    right[...] = jnp.concatenate(
        [jnp.concatenate([high, high], axis=1), jnp.concatenate([low, jnp.zeros_like(low)], axis=1)], axis=0
    )
    if mixed:
        own_ref, coef_ref = extra
        control[...] = sources[0][pl.ds(sources[0].shape[0] - control.shape[0], control.shape[0]), :]
    else:
        control[...] = extra[0][...].astype(jnp.float32)
    for source, (apart, span, begin, rows) in zip(sources, places):
        place = pl.ds(pl.multiple_of((who_ref[0] ^ apart) * span + begin, rows), rows)
        held[place, :] = source[pl.ds(0, rows), :] if mixed else source[0]

    @pl.loop(0, stride // 4)
    def _(step):
        for pair in range(2):
            first = step * 4 + pair * 2
            places = [pl.ds(first + side, LANES, stride=stride) for side in range(2)]
            value = jnp.concatenate([held[place, :] for place in places], axis=1)
            for place, piece in zip(places, left_gate(left_a[...], value)):
                held[place, :] = piece

    blocks = 4
    here = lax.broadcasted_iota(jnp.int32, (LANES, 2 * LANES), 0)
    there = lax.broadcasted_iota(jnp.int32, (LANES, 2 * LANES), 1)
    picked = there == 2 * here + half
    ones = jnp.ones((2 * LANES, LANES), jnp.bfloat16)
    for out, size in enumerate(sizes):
        target = targets[out]
        before = sum(sizes[:out])

        @pl.loop(0, size // (blocks * LANES))
        def _(step):
            begin = pl.multiple_of(step * (blocks * LANES), blocks * LANES)
            value = held[pl.ds(before + begin, blocks * LANES), :]
            acted = matmul_nt(jnp.concatenate(split_two(value), axis=1), right[...])
            acted = acted[:, :LANES] + acted[:, LANES:]
            chosen = []
            for block in range(blocks):
                at = (before // LANES + step * blocks + block) * 2
                row = jnp.concatenate([control[pl.ds(at, 1), :], control[pl.ds(at + 1, 1), :]], axis=1)
                chosen.append(jnp.where(picked, jnp.broadcast_to(row, picked.shape), 0.0))
            chosen = matmul(jnp.concatenate(chosen, axis=0).astype(jnp.bfloat16), ones)
            value = jnp.where(chosen > 0.5, acted, value)
            for block in range(0, blocks, 2):
                both = jnp.concatenate(
                    [value[(block + side) * LANES : (block + side + 1) * LANES] for side in range(2)], axis=1
                )
                for side, piece in enumerate(left_gate(left_b[...], both)):
                    place = pl.ds(begin + (block + side) * LANES, LANES)
                    if mixed:
                        piece = mix(coef_ref, 0, own_ref[place, :]) + mix(coef_ref, 2, piece)
                    target[place, :] = piece


def late(sources, places, gates, ctrl, who, half, sizes, *extra):
    mixed = len(extra) == 2
    total = sum(sizes)
    vmem = pl.BlockSpec(memory_space=pltpu.VMEM)
    smem = pl.BlockSpec(memory_space=pltpu.SMEM)
    source_specs = [
        vmem if mixed else pl.BlockSpec((1, *source.shape[1:]), lambda g: (half, 0, 0)) for source in sources
    ]
    gate_specs = [pl.BlockSpec((1, 2, LANES, LANES), lambda g, at=at: (at, 0, 0, 0)) for at in (2, 3)]
    return pl.pallas_call(
        functools.partial(late_kernel, half, places, sizes, mixed),
        grid=(1,),
        in_specs=source_specs + gate_specs + [vmem, smem] + ([vmem, smem] if mixed else [vmem]),
        out_specs=[vmem] * len(sizes),
        out_shape=[jax.ShapeDtypeStruct((size, LANES), jnp.float32) for size in sizes],
        scratch_shapes=[
            pltpu.VMEM((total, LANES), jnp.float32),
            pltpu.VMEM((total // HALF, LANES), jnp.float32),
            pltpu.VMEM((2 * LANES, 2 * LANES), jnp.bfloat16),
            pltpu.VMEM((2 * LANES, 2 * LANES), jnp.bfloat16),
            pltpu.VMEM((2 * LANES, 2 * LANES), jnp.bfloat16),
        ],
        compiler_params=pltpu.CompilerParams(vmem_limit_bytes=LATE_LIMIT),
        cost_estimate=COST,
        name="late",
    )(*sources, gates, gates, ctrl, who, *extra)


def final_kernel(zero_ref, own_ref, other_ref, coef_ref, *refs):
    out_ref = refs[-1]
    zero = zero_ref[...]
    one = mix(coef_ref, 0, own_ref[...]) + mix(coef_ref, 2, other_ref[...])
    lane = lax.broadcasted_iota(jnp.int32, zero.shape, 1)
    out_ref[0] = jnp.where(lane < HALF, zero, pltpu.roll(one, HALF, 1))
    out_ref[1] = jnp.where(lane < HALF, pltpu.roll(zero, HALF, 1), one)


def final(zero, own, other, coefs, before, carried):
    total, rows = zero.shape[0], own.shape[0]
    size = total // 8
    here = pl.BlockSpec((size, LANES), lambda g: (g, 0))
    return pl.pallas_call(
        final_kernel,
        grid=(rows // size,),
        in_specs=[
            pl.BlockSpec((size, LANES), lambda g: (before // size + g, 0)),
            here,
            here,
            pl.BlockSpec(memory_space=pltpu.SMEM),
        ]
        + [pl.BlockSpec(memory_space=pl.ANY)] * len(carried),
        out_specs=pl.BlockSpec((2, size, LANES), lambda g: (0, before // size + g, 0)),
        out_shape=jax.ShapeDtypeStruct((2, total, LANES), jnp.float32),
        input_output_aliases={4: 0} if carried else {},
        compiler_params=pltpu.CompilerParams(vmem_limit_bytes=FINAL_LIMIT),
        cost_estimate=COST,
        name="final",
    )(zero, own, other, coefs, *carried)


def coefficients(mid_angles, parity):
    cosine, sine = jnp.cos(mid_angles), jnp.sin(mid_angles)
    sign = (1 - 2 * parity).astype(jnp.float32)
    return jnp.stack(
        [cosine[0] * cosine[1], sign * (cosine[0] * sine[1]), -sign * (sine[0] * cosine[2]), -sine[0] * sine[2]]
    )


def after(value, *others):
    return lax.optimization_barrier((value, *others))[0]


def wide_ctrl(ctrl_gate):
    return jnp.block([[ctrl_gate[0], -ctrl_gate[1]], [ctrl_gate[1], ctrl_gate[0]]])


def body(amplitudes, layer_gates, ctrl_gate, control_mask, mid_angles):
    amount = amplitudes.shape[-1]
    total = amount // LANES
    groups = lax.axis_size("high")
    mid = lax.axis_size("mid")
    top_bit = mid.bit_length() - 2
    parity = lax.axis_index("mid") >> top_bit & 1
    who = lax.axis_index("high").astype(jnp.int32).reshape(1)

    def move(value, apart, across=1):
        pairs = [
            (high * mid + at, (high ^ apart) * mid + (at ^ across << top_bit))
            for high in range(groups)
            for at in range(mid)
        ]
        return lax.ppermute(value, ("high", "mid"), pairs)

    x = amplitudes.reshape(2, groups, total // groups // LANES, LANES, LANES)
    mask = control_mask.reshape(total // HALF, LANES)
    span = total // groups
    ctrl = wide_ctrl(ctrl_gate)
    coefs = coefficients(mid_angles, parity)
    places, away, pairs = [], [], []
    for apart in range(groups):
        chunks = 2 if apart < 2 and x.shape[2] % 2 == 0 else 1
        for chunk in range(chunks):
            part, pair = early(who, x, layer_gates, mask, apart, chunk, chunks)
            places.append((apart, span, chunk * (span // chunks), span // chunks))
            away.append(move(part, apart))
            pairs.append(pair)
    for at, (apart, *_) in enumerate(places):
        if apart == 1:
            pairs[at] = after(pairs[at], *[sent for sent, place in zip(away, places) if place[0] < 2])
        if apart:
            pairs[at] = move(pairs[at], apart, 0)
    sizes = [total // 8 * share for share in (2, 2, 2, 2)]
    own_one = late(pairs, places, layer_gates, ctrl, who, 1, sizes, mask)
    other_one = [move(piece, 0) for piece in own_one]
    (own_zero,) = late(pairs, places, layer_gates, ctrl, who, 0, [total], mask)
    (mixed,) = late(away, places, layer_gates, ctrl, who, 0, [total], own_zero, coefs)
    result = ()
    for at, size in enumerate(sizes):
        result = (final(mixed, own_one[at], other_one[at], coefs, sum(sizes[:at]), result),)
    return result[0].reshape(2, 1, 1, amount)


def solution(mesh):
    placed = (P(None, "high", "mid", None), P(), P(), P("high", "mid", None), P())
    return jax.shard_map(
        body, mesh=mesh, in_specs=placed, out_specs=P(None, "high", "mid", None), check_vma=False
    )
```

time: 207 us -> 198 us (0.957)
  Pallas kernels: 70.2 us -> 63.2 us
    pallas_call x11 -> x13, Pallas kernels: 70.2 us -> 63.2 us  [the longest x3 32 us: late(): pl.pallas_call(functools.partial(late_kernel, half, places, sizes, mixed)...]
    unnamed x24 -> x30, local copies, waits for them, and re-layouts: 5.93 us -> 3.96 us
    ppermute x11 -> x14, waiting for transfers between devices: 107 us -> 108 us  [move(): return lax.ppermute(value, ('high', 'mid'), pairs)]
    ppermute x11 -> x14, starting transfers between devices: 15.8 us -> 16 us  [move(): return lax.ppermute(value, ('high', 'mid'), pairs)]
  transfers between devices with their start and end apart: 11 -> 14, of which waited for: 7 -> 9; matrix products, arithmetic and copies ran while one was open for 1% -> 0% of each run, Pallas kernels for 31% -> 29%
where the time goes in v2:
time: 198 us; the launch traced here: 197 us
  waiting for transfers between devices  108 us (55%)
  Pallas kernels  63.2 us (32%)
  starting transfers between devices  16 us (8%)
  between operations  5.19 us (3%)
  local copies, waits for them, and re-layouts  4.69 us (2%)
    ppermute x14, waiting for transfers between devices, move(): return lax.ppermute(value, ('high', 'mid'), pairs)  108 us
    pallas_call x3, Pallas kernels, late(): pl.pallas_call(functools.partial(late_kernel, half, places, sizes, mixed)...  32 us
    pallas_call x6, Pallas kernels, early(): pl.pallas_call(functools.partial(early_kernel, tail), grid_spec=pltpu.Pre...  20.8 us
    ppermute x14, starting transfers between devices, move(): return lax.ppermute(value, ('high', 'mid'), pairs)  16 us
    pallas_call x4, Pallas kernels, final(): pl.pallas_call(final_kernel, grid=(rows // size,), in_specs=[pl.BlockSpec...  10.3 us
  transfers between devices with their start and end apart: 14, of which 9 were waited for; matrix products, arithmetic and copies ran while one was open for 0% of the time, Pallas kernels for 29%

profile of v2, /device:TPU:0, one launch (start us, length us, event | category | flops | bytes accessed | tf_op | source)
XLA Modules:
  0.0 197.1 jit_solution(2989751411178845016)
XLA Ops:
  0.0 3.1 %early.7 = (f32[512,128]{1,0:T(8,128)}, f32[2,512,128]{2,1,0:T(8,128)}) custom-call(s32[1]{0:T(128)} %bitcast.who_ref.refs_9_, f32[2,4,8,128,128]{4,3,2,1,0:T(8,128)} %bitcast.22, f32[4,2,128,128]{3,2,1,0:T(8,128)} %refs_7_.5, f32[4,2,128,128]{3,2,1,0:T(8,128)} %refs_7_.5, s32[64,128]{1,0:T(8,128)} %bitcast.14), custom_call_target="tpu_custom_call" | custom-call | flops 1 | bytes 1 | tf_op jit(solution)/shard_map/early/pallas_call | solution.py:80
  3.1 4.0 %collective-permute-start.1 = (f32[512,128]{1,0:T(8,128)}, f32[512,128]{1,0:T(8,128)}, u32[]{:S(2)}, u32[]{:S(2)}) collective-permute-start(f32[512,128]{1,0:T(8,128)} %get-tuple-element.24), channel_id=1, source_target_pairs={{0,4},{1,5},{2,6},{3,7},{4,0},{5,1},{6,2},{7,3},{8,12},{9,13},{10,... | collective-permute-start | bytes 786440 | tf_op jit(solution)/shard_map/ppermute | solution.py:267
  7.1 4.2 %early.10 = (f32[1024,128]{1,0:T(8,128)}, f32[2,1024,128]{2,1,0:T(8,128)}) custom-call(s32[1]{0:T(128)} %bitcast.who_ref.refs_9_, f32[2,4,8,128,128]{4,3,2,1,0:T(8,128)} %bitcast.23, f32[4,2,128,128]{3,2,1,0:T(8,128)} %refs_7_.5, f32[4,2,128,128]{3,2,1,0:T(8,128)} %refs_7_.5, s32[64,128]{1,0:T(8,128)} %bitcast.15), custom_call_target="tpu_custom_call" | custom-call | flops 1 | bytes 1 | tf_op jit(solution)/shard_map/early/pallas_call | solution.py:80
  11.3 1.5 collective-permute-start.8
  12.8 4.2 %early.11 = (f32[1024,128]{1,0:T(8,128)}, f32[2,1024,128]{2,1,0:T(8,128)}) custom-call(s32[1]{0:T(128)} %bitcast.who_ref.refs_9_, f32[2,4,8,128,128]{4,3,2,1,0:T(8,128)} %bitcast.24, f32[4,2,128,128]{3,2,1,0:T(8,128)} %refs_7_.5, f32[4,2,128,128]{3,2,1,0:T(8,128)} %refs_7_.5, s32[64,128]{1,0:T(8,128)} %bitcast.16), custom_call_target="tpu_custom_call" | custom-call | flops 1 | bytes 1 | tf_op jit(solution)/shard_map/early/pallas_call | solution.py:80
  17.0 3.1 %early.6 = (f32[576,128]{1,0:T(8,128)}, f32[2,512,128]{2,1,0:T(8,128)}) custom-call(s32[1]{0:T(128)} %bitcast.who_ref.refs_9_, f32[2,4,8,128,128]{4,3,2,1,0:T(8,128)} %bitcast.25, f32[4,2,128,128]{3,2,1,0:T(8,128)} %refs_7_.5, f32[4,2,128,128]{3,2,1,0:T(8,128)} %refs_7_.5, s32[64,128]{1,0:T(8,128)} %bitcast.17), custom_call_target="tpu_custom_call" | custom-call | flops 1 | bytes 1 | tf_op jit(solution)/shard_map/early/pallas_call | solution.py:80
  20.5 3.2 %early.8 = (f32[512,128]{1,0:T(8,128)}, f32[2,512,128]{2,1,0:T(8,128)}) custom-call(s32[1]{0:T(128)} %bitcast.who_ref.refs_9_, f32[2,4,8,128,128]{4,3,2,1,0:T(8,128)} %bitcast.26, f32[4,2,128,128]{3,2,1,0:T(8,128)} %refs_7_.5, f32[4,2,128,128]{3,2,1,0:T(8,128)} %refs_7_.5, s32[64,128]{1,0:T(8,128)} %bitcast.18), custom_call_target="tpu_custom_call" | custom-call | flops 1 | bytes 1 | tf_op jit(solution)/shard_map/early/pallas_call | solution.py:80
  23.8 2.4 %collective-permute-start.2 = (f32[512,128]{1,0:T(8,128)}, f32[512,128]{1,0:T(8,128)}, u32[]{:S(2)}, u32[]{:S(2)}) collective-permute-start(f32[512,128]{1,0:T(8,128)} %get-tuple-element.25), channel_id=1, source_target_pairs={{0,12},{1,13},{2,14},{3,15},{4,8},{5,9},{6,10},{7,11},{8,4},{9,5},... | collective-permute-start | bytes 786440 | tf_op jit(solution)/shard_map/ppermute | solution.py:267
  26.2 3.1 %early.9 = (f32[512,128]{1,0:T(8,128)}, f32[2,512,128]{2,1,0:T(8,128)}) custom-call(s32[1]{0:T(128)} %bitcast.who_ref.refs_9_, f32[2,4,8,128,128]{4,3,2,1,0:T(8,128)} %bitcast.27, f32[4,2,128,128]{3,2,1,0:T(8,128)} %refs_7_.5, f32[4,2,128,128]{3,2,1,0:T(8,128)} %refs_7_.5, s32[64,128]{1,0:T(8,128)} %bitcast.19), custom_call_target="tpu_custom_call" | custom-call | flops 1 | bytes 1 | tf_op jit(solution)/shard_map/early/pallas_call | solution.py:80
  29.5 24.4 %collective-permute-done.2.refs_2_ = f32[512,128]{1,0:T(8,128)} collective-permute-done((f32[512,128]{1,0:T(8,128)}, f32[512,128]{1,0:T(8,128)}, u32[]{:S(2)}, u32[]{:S(2)}) %collective-permute-start.2) | collective-permute-done | bytes 262176 | tf_op jit(solution)/shard_map/ppermute | solution.py:267
  54.1 16.5 %collective-permute-done.3.refs_3_ = f32[512,128]{1,0:T(8,128)S(1)} collective-permute-done((f32[512,128]{1,0:T(8,128)}, f32[512,128]{1,0:T(8,128)S(1)}, u32[]{:S(2)}, u32[]{:S(2)}) %collective-permute-start.3) | collective-permute-done | bytes 262176 | tf_op jit(solution)/shard_map/ppermute | solution.py:267
  71.2 1.5 collective-permute-done.6.refs_2_
  72.7 0.6 collective-permute-start.5
  73.5 10.7 %late.5 = (f32[1024,128]{1,0:T(8,128)}, f32[1024,128]{1,0:T(8,128)}, f32[1024,128]{1,0:T(8,128)}, f32[1024,128]{1,0:T(8,128)}) custom-call(f32[2,512,128]{2,1,0:T(8,128)S(1)} %copy-done.3, f32[2,512,128]{2,1,0:T(8,128)S(1)} %copy-done.2, f32[2,512,128]{2,1,0:T(8,128)S(1)} %collective-permute-done.6.refs_2_, ...), custom_call_target="tpu_custom_call" | custom-call | flops 1 | bytes 1 | tf_op jit(solution)/shard_map/late/pallas_call | solution.py:185
  84.3 3.1 %collective-permute-start.13 = (f32[1024,128]{1,0:T(8,128)}, f32[1024,128]{1,0:T(8,128)}, u32[]{:S(2)}, u32[]{:S(2)}) collective-permute-start(f32[1024,128]{1,0:T(8,128)} %get-tuple-element.40.own_ref), channel_id=1, source_target_pairs={{0,4},{1,5},{2,6},{3,7},{4,0},{5,1},{6,2},{7,3},{8,12},{9,13},{10,... | collective-permute-start | bytes 1572872 | tf_op jit(solution)/shard_map/ppermute | solution.py:267
  87.5 2.9 %collective-permute-start.11 = (f32[1024,128]{1,0:T(8,128)}, f32[1024,128]{1,0:T(8,128)}, u32[]{:S(2)}, u32[]{:S(2)}) collective-permute-start(f32[1024,128]{1,0:T(8,128)} %get-tuple-element.38.own_ref), channel_id=1, source_target_pairs={{0,4},{1,5},{2,6},{3,7},{4,0},{5,1},{6,2},{7,3},{8,12},{9,13},{10,... | collective-permute-start | bytes 1572872 | tf_op jit(solution)/shard_map/ppermute | solution.py:267
  90.3 37.1 %collective-permute-done.4.refs_4_ = f32[1024,128]{1,0:T(8,128)S(1)} collective-permute-done((f32[1024,128]{1,0:T(8,128)}, f32[1024,128]{1,0:T(8,128)S(1)}, u32[]{:S(2)}, u32[]{:S(2)}) %collective-permute-start.4) | collective-permute-done | bytes 524320 | tf_op jit(solution)/shard_map/ppermute | solution.py:267
  127.5 0.8 copy-done.9
  128.3 0.7 fusion.1
  134.1 1.0 copy-done.4
  135.2 1.0 copy-done.6
  136.2 1.0 copy-done.8
  137.3 9.8 %late.3.refs_10_ = f32[4096,128]{1,0:T(8,128)S(1)} custom-call(f32[2,512,128]{2,1,0:T(8,128)S(1)} %copy-done.4, f32[2,512,128]{2,1,0:T(8,128)S(1)} %copy-done.2, f32[2,512,128]{2,1,0:T(8,128)S(1)} %copy-done.6, f32[2,512,128]{2,1,0:T(8,128)S(1)} %copy-done.8, f32[2,1024,128]{2,1,0:T(8,128)S(1)} %collective-permute-done.8.refs_4_, ...), custom_call_target="tpu_custom_call" | custom-call | flops 1 | bytes 1 | tf_op jit(solution)/shard_map/late/pallas_call | solution.py:185
  147.0 3.6 %collective-permute-done.5.refs_5_ = f32[1024,128]{1,0:T(8,128)} collective-permute-done((f32[1024,128]{1,0:T(8,128)}, f32[1024,128]{1,0:T(8,128)}, u32[]{:S(2)}, u32[]{:S(2)}) %collective-permute-start.5) | collective-permute-done | bytes 524320 | tf_op jit(solution)/shard_map/ppermute | solution.py:267
  150.6 11.6 %late.4.zero_ref = f32[4096,128]{1,0:T(8,128)S(1)} custom-call(f32[576,128]{1,0:T(8,128)S(1)} %collective-permute-done.refs_0_, f32[512,128]{1,0:T(8,128)} %collective-permute-done.1.refs_1_, f32[512,128]{1,0:T(8,128)} %collective-permute-done.2.refs_2_, f32[512,128]{1,0:T(8,128)S(1)} %copy-done.12, f32[1024,128]{1,0:T(8,128)S(1)} %copy-done.10, ...), custom_call_target="tpu_custom_call" | custom-call | flops 1 | bytes 1 | tf_op jit(solution)/shard_map/late/pallas_call | solution.py:185
  162.2 2.6 %final.4.refs_0_ = f32[2,4096,128]{2,1,0:T(8,128)} custom-call(f32[4096,128]{1,0:T(8,128)S(1)} %late.4.zero_ref, f32[1024,128]{1,0:T(8,128)} %get-tuple-element.40.own_ref, f32[1024,128]{1,0:T(8,128)} %collective-permute-done.13.other_ref, f32[4]{0:T(128)S(1)} %pad_maximum_fusion.refs_11_.coef_ref), custom_call_target="tpu_custom_call" | custom-call | flops 1 | bytes 1 | tf_op jit(solution)/shard_map/final/pallas_call | solution.py:217
  164.8 7.6 %collective-permute-done.12.other_ref = f32[1024,128]{1,0:T(8,128)} collective-permute-done((f32[1024,128]{1,0:T(8,128)}, f32[1024,128]{1,0:T(8,128)}, u32[]{:S(2)}, u32[]{:S(2)}) %collective-permute-start.12) | collective-permute-done | bytes 524320 | tf_op jit(solution)/shard_map/ppermute | solution.py:267
  172.4 2.6 %final.5.refs_0_ = f32[2,4096,128]{2,1,0:T(8,128)} custom-call(f32[4096,128]{1,0:T(8,128)S(1)} %late.4.zero_ref, f32[1024,128]{1,0:T(8,128)} %get-tuple-element.39.own_ref, f32[1024,128]{1,0:T(8,128)} %collective-permute-done.12.other_ref, f32[4]{0:T(128)S(1)} %pad_maximum_fusion.refs_11_.coef_ref, ...), custom_call_target="tpu_custom_call", output_to_operand_aliasing={{}: (4, {})} | custom-call | flops 1 | bytes 1 | tf_op jit(solution)/shard_map/final/pallas_call | solution.py:217
  174.9 8.7 %collective-permute-done.11.other_ref = f32[1024,128]{1,0:T(8,128)} collective-permute-done((f32[1024,128]{1,0:T(8,128)}, f32[1024,128]{1,0:T(8,128)}, u32[]{:S(2)}, u32[]{:S(2)}) %collective-permute-start.11) | collective-permute-done | bytes 524320 | tf_op jit(solution)/shard_map/ppermute | solution.py:267
  183.6 2.6 %final.6.refs_0_ = f32[2,4096,128]{2,1,0:T(8,128)} custom-call(f32[4096,128]{1,0:T(8,128)S(1)} %late.4.zero_ref, f32[1024,128]{1,0:T(8,128)} %get-tuple-element.38.own_ref, f32[1024,128]{1,0:T(8,128)} %collective-permute-done.11.other_ref, f32[4]{0:T(128)S(1)} %pad_maximum_fusion.refs_11_.coef_ref, ...), custom_call_target="tpu_custom_call", output_to_operand_aliasing={{}: (4, {})} | custom-call | flops 1 | bytes 1 | tf_op jit(solution)/shard_map/final/pallas_call | solution.py:217
  186.2 8.4 %collective-permute-done.10.other_ref = f32[1024,128]{1,0:T(8,128)} collective-permute-done((f32[1024,128]{1,0:T(8,128)}, f32[1024,128]{1,0:T(8,128)}, u32[]{:S(2)}, u32[]{:S(2)}) %collective-permute-start.10) | collective-permute-done | bytes 524320 | tf_op jit(solution)/shard_map/ppermute | solution.py:267
  194.6 2.6 %final.7 = f32[2,4096,128]{2,1,0:T(8,128)} custom-call(f32[4096,128]{1,0:T(8,128)S(1)} %late.4.zero_ref, f32[1024,128]{1,0:T(8,128)} %get-tuple-element.37.own_ref, f32[1024,128]{1,0:T(8,128)} %collective-permute-done.10.other_ref, f32[4]{0:T(128)S(1)} %pad_maximum_fusion.refs_11_.coef_ref, f32[2,4096,128]{2,1,0:T(8,128)} %final.6.refs_0_), custom_call_target="tpu_custom_call", output_to_operand_aliasing={{}: (4, {})} | custom-call | flops 1 | bytes 1 | tf_op jit(solution)/shard_map/final/pallas_call | solution.py:217
  (45 shorter events, 1.8 us)
Async XLA Ops:
  3.1 26.2 %collective-permute-start.1 = (f32[512,128]{1,0:T(8,128)}, f32[512,128]{1,0:T(8,128)}, u32[]{:S(2)}, u32[]{:S(2)}) collective-permute-start(f32[512,128]{1,0:T(8,128)} %get-tuple-element.24), channel_id=1, source_target_pairs={{0,4},{1,5},{2,6},{3,7},{4,0},{5,1},{6,2},{7,3},{8,12},{9,13},{10,... | collective-permute-start | bytes 786440 | tf_op jit(solution)/shard_map/ppermute | solution.py:267
  11.3 62.2 %collective-permute-start.8 = (f32[2,1024,128]{2,1,0:T(8,128)}, f32[2,1024,128]{2,1,0:T(8,128)S(1)}, u32[]{:S(2)}, u32[]{:S(2)}) collective-permute-start(f32[2,1024,128]{2,1,0:T(8,128)} %get-tuple-element.35), channel_id=1, source_target_pairs={{0,16},{1,17},{2,18},{3,19},{4,20},{5,21},{6,22},{7,23},{8,24},{9,... | collective-permute-start | bytes 3145736 | tf_op jit(solution)/shard_map/ppermute | solution.py:267
  17.0 56.5 %collective-permute-start.9 = (f32[2,1024,128]{2,1,0:T(8,128)}, f32[2,1024,128]{2,1,0:T(8,128)S(1)}, u32[]{:S(2)}, u32[]{:S(2)}) collective-permute-start(f32[2,1024,128]{2,1,0:T(8,128)} %get-tuple-element.36), channel_id=1, source_target_pairs={{0,24},{1,25},{2,26},{3,27},{4,28},{5,29},{6,30},{7,31},{8,16},{9,... | collective-permute-start | bytes 3145736 | tf_op jit(solution)/shard_map/ppermute | solution.py:267
  20.1 51.0 %copy-start.13 = (f32[2,64,64]{2,1,0:T(8,128)S(1)}, f32[2,64,64]{2,1,0:T(8,128)}, u32[]{:S(2)}) copy-start(f32[2,64,64]{2,1,0:T(8,128)} %param.7) | copy-start | bytes 98308
  20.1 53.4 %copy-start = (f32[4,2,128,128]{3,2,1,0:T(8,128)S(1)}, f32[4,2,128,128]{3,2,1,0:T(8,128)}, u32[]{:S(2)}) copy-start(f32[4,2,128,128]{3,2,1,0:T(8,128)} %refs_7_.5) | copy-start | bytes 1572868
  20.1 53.4 %copy-start.1 = (s32[1,1,8192]{2,1,0:T(1,128)S(1)}, s32[1,1,8192]{2,1,0:T(1,128)}, u32[]{:S(2)}) copy-start(s32[1,1,8192]{2,1,0:T(1,128)} %param.8) | copy-start | bytes 98308
  20.1 53.4 %copy-start.2 = (f32[2,512,128]{2,1,0:T(8,128)S(1)}, f32[2,512,128]{2,1,0:T(8,128)}, u32[]{:S(2)}) copy-start(f32[2,512,128]{2,1,0:T(8,128)} %get-tuple-element.30.refs_1_) | copy-start | bytes 1572868
  20.1 53.4 %copy-start.3 = (f32[2,512,128]{2,1,0:T(8,128)S(1)}, f32[2,512,128]{2,1,0:T(8,128)}, u32[]{:S(2)}) copy-start(f32[2,512,128]{2,1,0:T(8,128)} %get-tuple-element.29.refs_0_) | copy-start | bytes 1572868
  20.1 50.5 %collective-permute-start = (f32[576,128]{1,0:T(8,128)}, f32[576,128]{1,0:T(8,128)S(1)}, u32[]{:S(2)}, u32[]{:S(2)}) collective-permute-start(f32[576,128]{1,0:T(8,128)} %get-tuple-element.23), channel_id=1, source_target_pairs={{0,4},{1,5},{2,6},{3,7},{4,0},{5,1},{6,2},{7,3},{8,12},{9,13},{10,... | collective-permute-start | bytes 884744 | tf_op jit(solution)/shard_map/ppermute | solution.py:267
  23.8 104.5 %copy-start.14 = (f32[3]{0:T(128)S(1)}, f32[3]{0:T(128)}, u32[]{:S(2)}) copy-start(f32[3]{0:T(128)} %param.9) | copy-start | bytes 40
  23.8 30.1 %collective-permute-start.2 = (f32[512,128]{1,0:T(8,128)}, f32[512,128]{1,0:T(8,128)}, u32[]{:S(2)}, u32[]{:S(2)}) collective-permute-start(f32[512,128]{1,0:T(8,128)} %get-tuple-element.25), channel_id=1, source_target_pairs={{0,12},{1,13},{2,14},{3,15},{4,8},{5,9},{6,10},{7,11},{8,4},{9,5},... | collective-permute-start | bytes 786440 | tf_op jit(solution)/shard_map/ppermute | solution.py:267
  29.3 41.3 %collective-permute-start.3 = (f32[512,128]{1,0:T(8,128)}, f32[512,128]{1,0:T(8,128)S(1)}, u32[]{:S(2)}, u32[]{:S(2)}) collective-permute-start(f32[512,128]{1,0:T(8,128)} %get-tuple-element.26), channel_id=1, source_target_pairs={{0,12},{1,13},{2,14},{3,15},{4,8},{5,9},{6,10},{7,11},{8,4},{9,5},... | collective-permute-start | bytes 786440 | tf_op jit(solution)/shard_map/ppermute | solution.py:267
  53.9 73.6 %collective-permute-start.4 = (f32[1024,128]{1,0:T(8,128)}, f32[1024,128]{1,0:T(8,128)S(1)}, u32[]{:S(2)}, u32[]{:S(2)}) collective-permute-start(f32[1024,128]{1,0:T(8,128)} %get-tuple-element.27), channel_id=1, source_target_pairs={{0,20},{1,21},{2,22},{3,23},{4,16},{5,17},{6,18},{7,19},{8,28},{9,... | collective-permute-start | bytes 1572872 | tf_op jit(solution)/shard_map/ppermute | solution.py:267
  70.6 56.9 %copy-start.11 = (f32[512,128]{1,0:T(8,128)}, f32[512,128]{1,0:T(8,128)S(1)}, u32[]{:S(2)}) copy-start(f32[512,128]{1,0:T(8,128)S(1)} %collective-permute-done.3.refs_3_) | copy-start | bytes 786436
  70.6 2.1 %collective-permute-start.6 = (f32[2,512,128]{2,1,0:T(8,128)}, f32[2,512,128]{2,1,0:T(8,128)S(1)}, u32[]{:S(2)}, u32[]{:S(2)}) collective-permute-start(f32[2,512,128]{2,1,0:T(8,128)} %get-tuple-element.32), channel_id=1, source_target_pairs={{0,8},{1,9},{2,10},{3,11},{4,12},{5,13},{6,14},{7,15},{8,0},{9,1},... | collective-permute-start | bytes 1572872 | tf_op jit(solution)/shard_map/ppermute | solution.py:267
  71.0 2.5 %collective-permute-start.7 = (f32[2,512,128]{2,1,0:T(8,128)}, f32[2,512,128]{2,1,0:T(8,128)S(1)}, u32[]{:S(2)}, u32[]{:S(2)}) collective-permute-start(f32[2,512,128]{2,1,0:T(8,128)} %get-tuple-element.34), channel_id=1, source_target_pairs={{0,8},{1,9},{2,10},{3,11},{4,12},{5,13},{6,14},{7,15},{8,0},{9,1},... | collective-permute-start | bytes 1572872 | tf_op jit(solution)/shard_map/ppermute | solution.py:267
  72.7 11.5 %copy-start.5 = (f32[2,512,128]{2,1,0:T(8,128)}, f32[2,512,128]{2,1,0:T(8,128)S(1)}, u32[]{:S(2)}) copy-start(f32[2,512,128]{2,1,0:T(8,128)S(1)} %collective-permute-done.6.refs_2_) | copy-start | bytes 1572868
  72.7 77.8 %collective-permute-start.5 = (f32[1024,128]{1,0:T(8,128)}, f32[1024,128]{1,0:T(8,128)}, u32[]{:S(2)}, u32[]{:S(2)}) collective-permute-start(f32[1024,128]{1,0:T(8,128)} %get-tuple-element.28), channel_id=1, source_target_pairs={{0,28},{1,29},{2,30},{3,31},{4,24},{5,25},{6,26},{7,27},{8,20},{9,... | collective-permute-start | bytes 1572872 | tf_op jit(solution)/shard_map/ppermute | solution.py:267
  73.5 10.8 %copy-start.7 = (f32[2,512,128]{2,1,0:T(8,128)}, f32[2,512,128]{2,1,0:T(8,128)S(1)}, u32[]{:S(2)}) copy-start(f32[2,512,128]{2,1,0:T(8,128)S(1)} %collective-permute-done.7.refs_3_) | copy-start | bytes 1572868
  84.3 77.9 %collective-permute-start.13 = (f32[1024,128]{1,0:T(8,128)}, f32[1024,128]{1,0:T(8,128)}, u32[]{:S(2)}, u32[]{:S(2)}) collective-permute-start(f32[1024,128]{1,0:T(8,128)} %get-tuple-element.40.own_ref), channel_id=1, source_target_pairs={{0,4},{1,5},{2,6},{3,7},{4,0},{5,1},{6,2},{7,3},{8,12},{9,13},{10,... | collective-permute-start | bytes 1572872 | tf_op jit(solution)/shard_map/ppermute | solution.py:267
  87.4 84.9 %collective-permute-start.12 = (f32[1024,128]{1,0:T(8,128)}, f32[1024,128]{1,0:T(8,128)}, u32[]{:S(2)}, u32[]{:S(2)}) collective-permute-start(f32[1024,128]{1,0:T(8,128)} %get-tuple-element.39.own_ref), channel_id=1, source_target_pairs={{0,4},{1,5},{2,6},{3,7},{4,0},{5,1},{6,2},{7,3},{8,12},{9,13},{10,... | collective-permute-start | bytes 1572872 | tf_op jit(solution)/shard_map/ppermute | solution.py:267
  87.5 96.1 %collective-permute-start.11 = (f32[1024,128]{1,0:T(8,128)}, f32[1024,128]{1,0:T(8,128)}, u32[]{:S(2)}, u32[]{:S(2)}) collective-permute-start(f32[1024,128]{1,0:T(8,128)} %get-tuple-element.38.own_ref), channel_id=1, source_target_pairs={{0,4},{1,5},{2,6},{3,7},{4,0},{5,1},{6,2},{7,3},{8,12},{9,13},{10,... | collective-permute-start | bytes 1572872 | tf_op jit(solution)/shard_map/ppermute | solution.py:267
  127.5 0.8 copy-start.9
  128.3 66.3 %collective-permute-start.10 = (f32[1024,128]{1,0:T(8,128)}, f32[1024,128]{1,0:T(8,128)}, u32[]{:S(2)}, u32[]{:S(2)}) collective-permute-start(f32[1024,128]{1,0:T(8,128)} %get-tuple-element.37.own_ref), channel_id=1, source_target_pairs={{0,4},{1,5},{2,6},{3,7},{4,0},{5,1},{6,2},{7,3},{8,12},{9,13},{10,... | collective-permute-start | bytes 1572872 | tf_op jit(solution)/shard_map/ppermute | solution.py:267
  134.1 1.0 copy-start.4
  135.2 1.0 copy-start.6
  136.2 1.0 copy-start.8
  137.3 13.3 %copy-start.10 = (f32[1024,128]{1,0:T(8,128)S(1)}, f32[1024,128]{1,0:T(8,128)}, u32[]{:S(2)}) copy-start(f32[1024,128]{1,0:T(8,128)} %copy-done.9) | copy-start | bytes 1572868
  137.3 13.3 %copy-start.12 = (f32[512,128]{1,0:T(8,128)S(1)}, f32[512,128]{1,0:T(8,128)}, u32[]{:S(2)}) copy-start(f32[512,128]{1,0:T(8,128)} %copy-done.11) | copy-start | bytes 786436

commit v3 on v2

--- a/solution.py
+++ b/solution.py
@@ -52,10 +52,19 @@
     return product[:, :LANES], product[:, LANES:]
 
 
-def early_kernel(tail, who_ref, x_ref, gate_a_ref, gate_b_ref, mask_ref, part_ref, pair_ref):
-    rows = pair_ref.shape[1]
+def selectors():
+    source = lax.broadcasted_iota(jnp.int32, (LANES, LANES), 0)
+    lane = lax.broadcasted_iota(jnp.int32, (LANES, LANES), 1)
+    return [(source == 2 * lane - shift).astype(jnp.bfloat16) for shift in (0, LANES)]
+
+
+def early_kernel(tail, who_ref, x_ref, gate_a_ref, gate_b_ref, mask_ref, part_ref, *pair_refs):
+    size = pair_refs[0].shape[1]
+    rows = size * len(pair_refs)
     if tail:
-        part_ref[pl.ds(rows, tail)] = mask_ref[...].astype(jnp.float32)
+        mask = mask_ref[...].astype(jnp.float32).astype(jnp.bfloat16)
+        near, far = selectors()
+        part_ref[pl.ds(rows, tail)] = matmul(mask[:tail], near) + matmul(mask[tail:], far)
     real, imag = gate_a_ref[0, 0], gate_a_ref[0, 1]
     pieces = []
     for begin in (0, HALF):
@@ -69,14 +78,14 @@
     for begin in range(0, rows, LANES):
         zero, one = left_gate(left, value[begin : begin + LANES])
         part_ref[pl.ds(begin, LANES)] = zero
-        pair_ref[0, pl.ds(begin, LANES)] = zero
-        pair_ref[1, pl.ds(begin, LANES)] = one
-
-
-def early(who, x, gates, mask, apart, chunk, chunks):
+        pair_refs[begin // size][0, pl.ds(begin % size, LANES)] = zero
+        pair_refs[begin // size][1, pl.ds(begin % size, LANES)] = one
+
+
+def early(who, x, gates, mask, apart, chunk, chunks, carrier, pieces):
     blocks = x.shape[2] // chunks
     rows = blocks * LANES
-    tail = mask.shape[0] if apart == 0 and chunk == 0 else 0
+    tail = mask.shape[0] // 2 if carrier else 0
     return pl.pallas_call(
         functools.partial(early_kernel, tail),
         grid_spec=pltpu.PrefetchScalarGridSpec(
@@ -90,13 +99,13 @@
             ],
             out_specs=[
                 pl.BlockSpec((rows + tail, LANES), lambda g, who: (0, 0)),
-                pl.BlockSpec((2, rows, LANES), lambda g, who: (0, 0, 0)),
-            ],
+            ]
+            + [pl.BlockSpec((2, rows // pieces, LANES), lambda g, who: (0, 0, 0))] * pieces,
         ),
         out_shape=[
             jax.ShapeDtypeStruct((rows + tail, LANES), jnp.float32),
-            jax.ShapeDtypeStruct((2, rows, LANES), jnp.float32),
-        ],
+        ]
+        + [jax.ShapeDtypeStruct((2, rows // pieces, LANES), jnp.float32)] * pieces,
         compiler_params=pltpu.CompilerParams(vmem_limit_bytes=EARLY_LIMIT),
         cost_estimate=COST,
         name="early",
@@ -124,7 +133,14 @@
     )
     if mixed:
         own_ref, coef_ref = extra
-        control[...] = sources[0][pl.ds(sources[0].shape[0] - control.shape[0], control.shape[0]), :]
+        tail = control.shape[0] // 2
+        (packed,) = [
+            source[pl.ds(place[3], tail), :].astype(jnp.bfloat16)
+            for source, place in zip(sources, places)
+            if source.shape[0] > place[3]
+        ]
+        for at, selector in enumerate(selectors()):
+            control[pl.ds(at * tail, tail)] = matmul_nt(packed, selector)
     else:
         control[...] = extra[0][...].astype(jnp.float32)
     for source, (apart, span, begin, rows) in zip(sources, places):
@@ -271,24 +287,30 @@
     span = total // groups
     ctrl = wide_ctrl(ctrl_gate)
     coefs = coefficients(mid_angles, parity)
-    places, away, pairs = [], [], []
+    away, away_places, pairs, pair_places = [], [], [], []
     for apart in range(groups):
-        chunks = 2 if apart < 2 and x.shape[2] % 2 == 0 else 1
+        chunks = 1
+        pieces = 2 // chunks if apart == 1 and x.shape[2] % 2 == 0 else 1
+        size = span // chunks
         for chunk in range(chunks):
-            part, pair = early(who, x, layer_gates, mask, apart, chunk, chunks)
-            places.append((apart, span, chunk * (span // chunks), span // chunks))
+            carrier = apart == 0
+            part, *both = early(who, x, layer_gates, mask, apart, chunk, chunks, carrier, pieces)
             away.append(move(part, apart))
-            pairs.append(pair)
-    for at, (apart, *_) in enumerate(places):
+            away_places.append((apart, span, chunk * size, size))
+            for piece, pair in enumerate(both):
+                pairs.append(pair)
+                pair_places.append((apart, span, chunk * size + piece * (size // pieces), size // pieces))
+    first = [sent for sent, place in zip(away, away_places) if place[0] < 2]
+    for at, (apart, *_) in enumerate(pair_places):
         if apart == 1:
-            pairs[at] = after(pairs[at], *[sent for sent, place in zip(away, places) if place[0] < 2])
+            pairs[at] = after(pairs[at], *first)
         if apart:
             pairs[at] = move(pairs[at], apart, 0)
     sizes = [total // 8 * share for share in (2, 2, 2, 2)]
-    own_one = late(pairs, places, layer_gates, ctrl, who, 1, sizes, mask)
+    own_one = late(pairs, pair_places, layer_gates, ctrl, who, 1, sizes, mask)
     other_one = [move(piece, 0) for piece in own_one]
-    (own_zero,) = late(pairs, places, layer_gates, ctrl, who, 0, [total], mask)
-    (mixed,) = late(away, places, layer_gates, ctrl, who, 0, [total], own_zero, coefs)
+    (own_zero,) = late(pairs, pair_places, layer_gates, ctrl, who, 0, [total], mask)
+    (mixed,) = late(away, away_places, layer_gates, ctrl, who, 0, [total], own_zero, coefs)
     result = ()
     for at, size in enumerate(sizes):
         result = (final(mixed, own_one[at], other_one[at], coefs, sum(sizes[:at]), result),)

time: 198 us -> 196 us (0.990)
  starting transfers between devices: 16 us -> 35 us
  waiting for transfers between devices: 108 us -> 90.3 us
  Pallas kernels: 63.2 us -> 58.9 us
    ppermute x14 -> x12, starting transfers between devices: 16 us -> 35 us  [move(): return lax.ppermute(value, ('high', 'mid'), pairs)]
    ppermute x14 -> x12, waiting for transfers between devices: 108 us -> 90.3 us  [move(): return lax.ppermute(value, ('high', 'mid'), pairs)]
    pallas_call x6 -> x4, Pallas kernels: 20.8 us -> 16.7 us  [early(): pl.pallas_call(functools.partial(early_kernel, tail), grid_spec=pltpu.Pre...]
  transfers between devices with their start and end apart: 14 -> 12, of which waited for: 9 -> 7; matrix products, arithmetic and copies ran while one was open for 0% -> 0% of each run, Pallas kernels for 29% -> 27%
where the time goes in v3:
time: 196 us; the launch traced here: 195 us
  waiting for transfers between devices  90.3 us (46%)
  Pallas kernels  58.9 us (30%)
  starting transfers between devices  35 us (18%)
  local copies, waits for them, and re-layouts  5.58 us (3%)
  between operations  5.26 us (3%)
    ppermute x12, waiting for transfers between devices, move(): return lax.ppermute(value, ('high', 'mid'), pairs)  90.3 us
    ppermute x12, starting transfers between devices, move(): return lax.ppermute(value, ('high', 'mid'), pairs)  35 us
    pallas_call x3, Pallas kernels, late(): pl.pallas_call(functools.partial(late_kernel, half, places, sizes, mixed)...  32 us
    pallas_call x4, Pallas kernels, early(): pl.pallas_call(functools.partial(early_kernel, tail), grid_spec=pltpu.Pre...  16.7 us
    pallas_call x4, Pallas kernels, final(): pl.pallas_call(final_kernel, grid=(rows // size,), in_specs=[pl.BlockSpec...  10.3 us
    unnamed x30, local copies, waits for them, and re-layouts  4.84 us
  transfers between devices with their start and end apart: 12, of which 7 were waited for; matrix products, arithmetic and copies ran while one was open for 0% of the time, Pallas kernels for 27%

profile of v3, /device:TPU:0, one launch (start us, length us, event | category | flops | bytes accessed | tf_op | source)
XLA Modules:
  0.0 195.2 jit_solution(15593667391365399870)
XLA Ops:
  0.0 4.2 %early.4 = (f32[1056,128]{1,0:T(8,128)}, f32[2,1024,128]{2,1,0:T(8,128)}) custom-call(s32[1]{0:T(128)} %bitcast.who_ref.refs_8_.refs_7_, f32[2,4,8,128,128]{4,3,2,1,0:T(8,128)} %bitcast.20, f32[4,2,128,128]{3,2,1,0:T(8,128)} %refs_6_.3, f32[4,2,128,128]{3,2,1,0:T(8,128)} %refs_6_.3, s32[64,128]{1,0:T(8,128)} %bitcast.14), custom_call_target="tpu_custom_call" | custom-call | flops 1 | bytes 1 | tf_op jit(solution)/shard_map/early/pallas_call | solution.py:89
  4.2 4.0 %collective-permute-start = (f32[1056,128]{1,0:T(8,128)}, f32[1056,128]{1,0:T(8,128)S(1)}, u32[]{:S(2)}, u32[]{:S(2)}) collective-permute-start(f32[1056,128]{1,0:T(8,128)} %get-tuple-element.20), channel_id=1, source_target_pairs={{0,4},{1,5},{2,6},{3,7},{4,0},{5,1},{6,2},{7,3},{8,12},{9,13},{10,... | collective-permute-start | bytes 1622024 | tf_op jit(solution)/shard_map/ppermute | solution.py:283
  8.2 4.0 %early.5 = (f32[1024,128]{1,0:T(8,128)}, f32[2,512,128]{2,1,0:T(8,128)}, f32[2,512,128]{2,1,0:T(8,128)}) custom-call(s32[1]{0:T(128)} %bitcast.who_ref.refs_8_.refs_7_, f32[2,4,8,128,128]{4,3,2,1,0:T(8,128)} %bitcast.21, f32[4,2,128,128]{3,2,1,0:T(8,128)} %refs_6_.3, f32[4,2,128,128]{3,2,1,0:T(8,128)} %refs_6_.3, s32[64,128]{1,0:T(8,128)} %bitcast.15), custom_call_target="tpu_custom_call" | custom-call | flops 1 | bytes 1 | tf_op jit(solution)/shard_map/early/pallas_call | solution.py:89
  12.3 4.3 %early.6 = (f32[1024,128]{1,0:T(8,128)}, f32[2,1024,128]{2,1,0:T(8,128)}) custom-call(s32[1]{0:T(128)} %bitcast.who_ref.refs_8_.refs_7_, f32[2,4,8,128,128]{4,3,2,1,0:T(8,128)} %bitcast.22, f32[4,2,128,128]{3,2,1,0:T(8,128)} %refs_6_.3, f32[4,2,128,128]{3,2,1,0:T(8,128)} %refs_6_.3, s32[64,128]{1,0:T(8,128)} %bitcast.16), custom_call_target="tpu_custom_call" | custom-call | flops 1 | bytes 1 | tf_op jit(solution)/shard_map/early/pallas_call | solution.py:89
  16.6 1.5 collective-permute-start.6
  18.1 4.2 %early.7 = (f32[1024,128]{1,0:T(8,128)}, f32[2,1024,128]{2,1,0:T(8,128)}) custom-call(s32[1]{0:T(128)} %bitcast.who_ref.refs_8_.refs_7_, f32[2,4,8,128,128]{4,3,2,1,0:T(8,128)} %bitcast.23, f32[4,2,128,128]{3,2,1,0:T(8,128)} %refs_6_.3, f32[4,2,128,128]{3,2,1,0:T(8,128)} %refs_6_.3, s32[64,128]{1,0:T(8,128)} %bitcast.17), custom_call_target="tpu_custom_call" | custom-call | flops 1 | bytes 1 | tf_op jit(solution)/shard_map/early/pallas_call | solution.py:89
  22.3 3.7 %collective-permute-start.2 = (f32[1024,128]{1,0:T(8,128)}, f32[1024,128]{1,0:T(8,128)S(1)}, u32[]{:S(2)}, u32[]{:S(2)}) collective-permute-start(f32[1024,128]{1,0:T(8,128)} %get-tuple-element.22), channel_id=1, source_target_pairs={{0,20},{1,21},{2,22},{3,23},{4,16},{5,17},{6,18},{7,19},{8,28},{9,... | collective-permute-start | bytes 1572872 | tf_op jit(solution)/shard_map/ppermute | solution.py:283
  26.0 39.1 %collective-permute-done.1.refs_1_ = f32[1024,128]{1,0:T(8,128)S(1)} collective-permute-done((f32[1024,128]{1,0:T(8,128)}, f32[1024,128]{1,0:T(8,128)S(1)}, u32[]{:S(2)}, u32[]{:S(2)}) %collective-permute-start.1) | collective-permute-done | bytes 524320 | tf_op jit(solution)/shard_map/ppermute | solution.py:283
  65.2 0.8 copy-done.9
  65.9 1.5 collective-permute-start.4
  67.5 0.1 maximum_maximum_fusion.refs_7_.refs_6_
  67.6 1.3 collective-permute-start.3
  68.9 0.2 collective-permute-done.4.refs_1_
  69.2 0.7 collective-permute-done.5.refs_2_
  69.9 10.7 %late.5 = (f32[1024,128]{1,0:T(8,128)}, f32[1024,128]{1,0:T(8,128)}, f32[1024,128]{1,0:T(8,128)}, f32[1024,128]{1,0:T(8,128)}) custom-call(f32[2,1024,128]{2,1,0:T(8,128)S(1)} %copy-done.1, f32[2,512,128]{2,1,0:T(8,128)S(1)} %collective-permute-done.4.refs_1_, f32[2,512,128]{2,1,0:T(8,128)S(1)} %collective-permute-done.5.refs_2_, ...), custom_call_target="tpu_custom_call" | custom-call | flops 1 | bytes 1 | tf_op jit(solution)/shard_map/late/pallas_call | solution.py:201
  80.7 1.0 copy-done.2
  81.7 19.8 %collective-permute-start.11 = (f32[1024,128]{1,0:T(8,128)}, f32[1024,128]{1,0:T(8,128)}, u32[]{:S(2)}, u32[]{:S(2)}) collective-permute-start(f32[1024,128]{1,0:T(8,128)} %get-tuple-element.34.own_ref), channel_id=1, source_target_pairs={{0,4},{1,5},{2,6},{3,7},{4,0},{5,1},{6,2},{7,3},{8,12},{9,13},{10,... | collective-permute-start | bytes 1572872 | tf_op jit(solution)/shard_map/ppermute | solution.py:283
  101.5 2.9 %collective-permute-start.9 = (f32[1024,128]{1,0:T(8,128)}, f32[1024,128]{1,0:T(8,128)}, u32[]{:S(2)}, u32[]{:S(2)}) collective-permute-start(f32[1024,128]{1,0:T(8,128)} %get-tuple-element.32.own_ref), channel_id=1, source_target_pairs={{0,4},{1,5},{2,6},{3,7},{4,0},{5,1},{6,2},{7,3},{8,12},{9,13},{10,... | collective-permute-start | bytes 1572872 | tf_op jit(solution)/shard_map/ppermute | solution.py:283
  104.4 0.8 copy-done.11
  105.3 0.7 fusion.1
  111.2 1.2 copy-done.3
  112.4 1.0 copy-done.5
  113.4 9.8 %late.3.refs_8_ = f32[4096,128]{1,0:T(8,128)S(1)} custom-call(f32[2,1024,128]{2,1,0:T(8,128)S(1)} %copy-done.1, f32[2,512,128]{2,1,0:T(8,128)S(1)} %collective-permute-done.4.refs_1_, f32[2,512,128]{2,1,0:T(8,128)S(1)} %copy-done.5, f32[2,1024,128]{2,1,0:T(8,128)S(1)} %collective-permute-done.6.refs_3_, f32[2,1024,128]{2,1,0:T(8,128)S(1)} %copy-done.3, ...), custom_call_target="tpu_custom_call" | custom-call | flops 1 | bytes 1 | tf_op jit(solution)/shard_map/late/pallas_call | solution.py:201
  123.3 11.5 %late.4.zero_ref = f32[4096,128]{1,0:T(8,128)S(1)} custom-call(f32[1056,128]{1,0:T(8,128)S(1)} %copy-done.8, f32[1024,128]{1,0:T(8,128)S(1)} %copy-done.10, f32[1024,128]{1,0:T(8,128)S(1)} %copy-done.12, f32[1024,128]{1,0:T(8,128)} %collective-permute-done.3.refs_3_, f32[4,2,128,128]{3,2,1,0:T(8,128)S(1)} %copy-done, f32[4,2,128,128]{3,2,1,0:T(8,128)S(1)} %copy-done, ...), custom_call_target="tpu_custom_call" | custom-call | flops 1 | bytes 1 | tf_op jit(solution)/shard_map/late/pallas_call | solution.py:201
  134.7 24.7 %collective-permute-done.11.other_ref = f32[1024,128]{1,0:T(8,128)} collective-permute-done((f32[1024,128]{1,0:T(8,128)}, f32[1024,128]{1,0:T(8,128)}, u32[]{:S(2)}, u32[]{:S(2)}) %collective-permute-start.11) | collective-permute-done | bytes 524320 | tf_op jit(solution)/shard_map/ppermute | solution.py:283
  159.4 2.6 %final.4.refs_0_ = f32[2,4096,128]{2,1,0:T(8,128)} custom-call(f32[4096,128]{1,0:T(8,128)S(1)} %late.4.zero_ref, f32[1024,128]{1,0:T(8,128)} %get-tuple-element.34.own_ref, f32[1024,128]{1,0:T(8,128)} %collective-permute-done.11.other_ref, f32[4]{0:T(128)S(1)} %pad_maximum_fusion.refs_9_.coef_ref), custom_call_target="tpu_custom_call" | custom-call | flops 1 | bytes 1 | tf_op jit(solution)/shard_map/final/pallas_call | solution.py:233
  162.0 8.7 %collective-permute-done.10.other_ref = f32[1024,128]{1,0:T(8,128)} collective-permute-done((f32[1024,128]{1,0:T(8,128)}, f32[1024,128]{1,0:T(8,128)}, u32[]{:S(2)}, u32[]{:S(2)}) %collective-permute-start.10) | collective-permute-done | bytes 524320 | tf_op jit(solution)/shard_map/ppermute | solution.py:283
  170.7 2.6 %final.5.refs_0_ = f32[2,4096,128]{2,1,0:T(8,128)} custom-call(f32[4096,128]{1,0:T(8,128)S(1)} %late.4.zero_ref, f32[1024,128]{1,0:T(8,128)} %get-tuple-element.33.own_ref, f32[1024,128]{1,0:T(8,128)} %collective-permute-done.10.other_ref, f32[4]{0:T(128)S(1)} %pad_maximum_fusion.refs_9_.coef_ref, ...), custom_call_target="tpu_custom_call", output_to_operand_aliasing={{}: (4, {})} | custom-call | flops 1 | bytes 1 | tf_op jit(solution)/shard_map/final/pallas_call | solution.py:233
  173.2 8.7 %collective-permute-done.9.other_ref = f32[1024,128]{1,0:T(8,128)} collective-permute-done((f32[1024,128]{1,0:T(8,128)}, f32[1024,128]{1,0:T(8,128)}, u32[]{:S(2)}, u32[]{:S(2)}) %collective-permute-start.9) | collective-permute-done | bytes 524320 | tf_op jit(solution)/shard_map/ppermute | solution.py:283
  181.9 2.6 %final.6.refs_0_ = f32[2,4096,128]{2,1,0:T(8,128)} custom-call(f32[4096,128]{1,0:T(8,128)S(1)} %late.4.zero_ref, f32[1024,128]{1,0:T(8,128)} %get-tuple-element.32.own_ref, f32[1024,128]{1,0:T(8,128)} %collective-permute-done.9.other_ref, f32[4]{0:T(128)S(1)} %pad_maximum_fusion.refs_9_.coef_ref, ...), custom_call_target="tpu_custom_call", output_to_operand_aliasing={{}: (4, {})} | custom-call | flops 1 | bytes 1 | tf_op jit(solution)/shard_map/final/pallas_call | solution.py:233
  184.5 8.2 %collective-permute-done.8.other_ref = f32[1024,128]{1,0:T(8,128)} collective-permute-done((f32[1024,128]{1,0:T(8,128)}, f32[1024,128]{1,0:T(8,128)}, u32[]{:S(2)}, u32[]{:S(2)}) %collective-permute-start.8) | collective-permute-done | bytes 524320 | tf_op jit(solution)/shard_map/ppermute | solution.py:283
  192.7 2.6 %final.7 = f32[2,4096,128]{2,1,0:T(8,128)} custom-call(f32[4096,128]{1,0:T(8,128)S(1)} %late.4.zero_ref, f32[1024,128]{1,0:T(8,128)} %get-tuple-element.31.own_ref, f32[1024,128]{1,0:T(8,128)} %collective-permute-done.8.other_ref, f32[4]{0:T(128)S(1)} %pad_maximum_fusion.refs_9_.coef_ref, f32[2,4096,128]{2,1,0:T(8,128)} %final.6.refs_0_), custom_call_target="tpu_custom_call", output_to_operand_aliasing={{}: (4, {})} | custom-call | flops 1 | bytes 1 | tf_op jit(solution)/shard_map/final/pallas_call | solution.py:233
  (39 shorter events, 0.4 us)
Async XLA Ops:
  4.2 61.8 %collective-permute-start = (f32[1056,128]{1,0:T(8,128)}, f32[1056,128]{1,0:T(8,128)S(1)}, u32[]{:S(2)}, u32[]{:S(2)}) collective-permute-start(f32[1056,128]{1,0:T(8,128)} %get-tuple-element.20), channel_id=1, source_target_pairs={{0,4},{1,5},{2,6},{3,7},{4,0},{5,1},{6,2},{7,3},{8,12},{9,13},{10,... | collective-permute-start | bytes 1622024 | tf_op jit(solution)/shard_map/ppermute | solution.py:283
  12.2 55.3 %copy-start.13 = (f32[2,64,64]{2,1,0:T(8,128)S(1)}, f32[2,64,64]{2,1,0:T(8,128)}, u32[]{:S(2)}) copy-start(f32[2,64,64]{2,1,0:T(8,128)} %param.7) | copy-start | bytes 98308
  12.2 57.7 %copy-start = (f32[4,2,128,128]{3,2,1,0:T(8,128)S(1)}, f32[4,2,128,128]{3,2,1,0:T(8,128)}, u32[]{:S(2)}) copy-start(f32[4,2,128,128]{3,2,1,0:T(8,128)} %refs_6_.3) | copy-start | bytes 1572868
  12.2 57.7 %copy-start.1 = (f32[2,1024,128]{2,1,0:T(8,128)S(1)}, f32[2,1024,128]{2,1,0:T(8,128)}, u32[]{:S(2)}) copy-start(f32[2,1024,128]{2,1,0:T(8,128)} %get-tuple-element.24.refs_0_) | copy-start | bytes 3145732
  12.2 57.7 %copy-start.6 = (s32[1,1,8192]{2,1,0:T(1,128)S(1)}, s32[1,1,8192]{2,1,0:T(1,128)}, u32[]{:S(2)}) copy-start(s32[1,1,8192]{2,1,0:T(1,128)} %param.8) | copy-start | bytes 98308
  12.2 52.9 %collective-permute-start.1 = (f32[1024,128]{1,0:T(8,128)}, f32[1024,128]{1,0:T(8,128)S(1)}, u32[]{:S(2)}, u32[]{:S(2)}) collective-permute-start(f32[1024,128]{1,0:T(8,128)} %get-tuple-element.21), channel_id=1, source_target_pairs={{0,12},{1,13},{2,14},{3,15},{4,8},{5,9},{6,10},{7,11},{8,4},{9,5},... | collective-permute-start | bytes 1572872 | tf_op jit(solution)/shard_map/ppermute | solution.py:283
  16.6 88.6 %copy-start.14 = (f32[3]{0:T(128)S(1)}, f32[3]{0:T(128)}, u32[]{:S(2)}) copy-start(f32[3]{0:T(128)} %param.9) | copy-start | bytes 40
  16.6 51.0 %collective-permute-start.6 = (f32[2,1024,128]{2,1,0:T(8,128)}, f32[2,1024,128]{2,1,0:T(8,128)S(1)}, u32[]{:S(2)}, u32[]{:S(2)}) collective-permute-start(f32[2,1024,128]{2,1,0:T(8,128)} %get-tuple-element.29), channel_id=1, source_target_pairs={{0,16},{1,17},{2,18},{3,19},{4,20},{5,21},{6,22},{7,23},{8,24},{9,... | collective-permute-start | bytes 3145736 | tf_op jit(solution)/shard_map/ppermute | solution.py:283
  22.3 46.6 %collective-permute-start.7 = (f32[2,1024,128]{2,1,0:T(8,128)}, f32[2,1024,128]{2,1,0:T(8,128)S(1)}, u32[]{:S(2)}, u32[]{:S(2)}) collective-permute-start(f32[2,1024,128]{2,1,0:T(8,128)} %get-tuple-element.30), channel_id=1, source_target_pairs={{0,24},{1,25},{2,26},{3,27},{4,28},{5,29},{6,30},{7,31},{8,16},{9,... | collective-permute-start | bytes 3145736 | tf_op jit(solution)/shard_map/ppermute | solution.py:283
  22.3 82.1 %collective-permute-start.2 = (f32[1024,128]{1,0:T(8,128)}, f32[1024,128]{1,0:T(8,128)S(1)}, u32[]{:S(2)}, u32[]{:S(2)}) collective-permute-start(f32[1024,128]{1,0:T(8,128)} %get-tuple-element.22), channel_id=1, source_target_pairs={{0,20},{1,21},{2,22},{3,23},{4,16},{5,17},{6,18},{7,19},{8,28},{9,... | collective-permute-start | bytes 1572872 | tf_op jit(solution)/shard_map/ppermute | solution.py:283
  65.2 0.8 copy-start.9
  65.9 15.7 %copy-start.7 = (f32[1056,128]{1,0:T(8,128)}, f32[1056,128]{1,0:T(8,128)S(1)}, u32[]{:S(2)}) copy-start(f32[1056,128]{1,0:T(8,128)S(1)} %collective-permute-done.refs_0_) | copy-start | bytes 1622020
  65.9 3.2 %collective-permute-start.4 = (f32[2,512,128]{2,1,0:T(8,128)}, f32[2,512,128]{2,1,0:T(8,128)S(1)}, u32[]{:S(2)}, u32[]{:S(2)}) collective-permute-start(f32[2,512,128]{2,1,0:T(8,128)} %get-tuple-element.26), channel_id=1, source_target_pairs={{0,8},{1,9},{2,10},{3,11},{4,12},{5,13},{6,14},{7,15},{8,0},{9,1},... | collective-permute-start | bytes 1572872 | tf_op jit(solution)/shard_map/ppermute | solution.py:283
  67.4 2.5 %collective-permute-start.5 = (f32[2,512,128]{2,1,0:T(8,128)}, f32[2,512,128]{2,1,0:T(8,128)S(1)}, u32[]{:S(2)}, u32[]{:S(2)}) collective-permute-start(f32[2,512,128]{2,1,0:T(8,128)} %get-tuple-element.28), channel_id=1, source_target_pairs={{0,8},{1,9},{2,10},{3,11},{4,12},{5,13},{6,14},{7,15},{8,0},{9,1},... | collective-permute-start | bytes 1572872 | tf_op jit(solution)/shard_map/ppermute | solution.py:283
  67.6 55.6 %collective-permute-start.3 = (f32[1024,128]{1,0:T(8,128)}, f32[1024,128]{1,0:T(8,128)}, u32[]{:S(2)}, u32[]{:S(2)}) collective-permute-start(f32[1024,128]{1,0:T(8,128)} %get-tuple-element.23), channel_id=1, source_target_pairs={{0,28},{1,29},{2,30},{3,31},{4,24},{5,25},{6,26},{7,27},{8,20},{9,... | collective-permute-start | bytes 1572872 | tf_op jit(solution)/shard_map/ppermute | solution.py:283
  69.9 10.8 %copy-start.4 = (f32[2,512,128]{2,1,0:T(8,128)}, f32[2,512,128]{2,1,0:T(8,128)S(1)}, u32[]{:S(2)}) copy-start(f32[2,512,128]{2,1,0:T(8,128)S(1)} %collective-permute-done.5.refs_2_) | copy-start | bytes 1572868
  80.7 1.0 copy-start.2
  81.7 77.8 %collective-permute-start.11 = (f32[1024,128]{1,0:T(8,128)}, f32[1024,128]{1,0:T(8,128)}, u32[]{:S(2)}, u32[]{:S(2)}) collective-permute-start(f32[1024,128]{1,0:T(8,128)} %get-tuple-element.34.own_ref), channel_id=1, source_target_pairs={{0,4},{1,5},{2,6},{3,7},{4,0},{5,1},{6,2},{7,3},{8,12},{9,13},{10,... | collective-permute-start | bytes 1572872 | tf_op jit(solution)/shard_map/ppermute | solution.py:283
  101.5 69.2 %collective-permute-start.10 = (f32[1024,128]{1,0:T(8,128)}, f32[1024,128]{1,0:T(8,128)}, u32[]{:S(2)}, u32[]{:S(2)}) collective-permute-start(f32[1024,128]{1,0:T(8,128)} %get-tuple-element.33.own_ref), channel_id=1, source_target_pairs={{0,4},{1,5},{2,6},{3,7},{4,0},{5,1},{6,2},{7,3},{8,12},{9,13},{10,... | collective-permute-start | bytes 1572872 | tf_op jit(solution)/shard_map/ppermute | solution.py:283
  101.5 80.4 %collective-permute-start.9 = (f32[1024,128]{1,0:T(8,128)}, f32[1024,128]{1,0:T(8,128)}, u32[]{:S(2)}, u32[]{:S(2)}) collective-permute-start(f32[1024,128]{1,0:T(8,128)} %get-tuple-element.32.own_ref), channel_id=1, source_target_pairs={{0,4},{1,5},{2,6},{3,7},{4,0},{5,1},{6,2},{7,3},{8,12},{9,13},{10,... | collective-permute-start | bytes 1572872 | tf_op jit(solution)/shard_map/ppermute | solution.py:283
  104.4 0.8 copy-start.11
  105.2 87.5 %collective-permute-start.8 = (f32[1024,128]{1,0:T(8,128)}, f32[1024,128]{1,0:T(8,128)}, u32[]{:S(2)}, u32[]{:S(2)}) collective-permute-start(f32[1024,128]{1,0:T(8,128)} %get-tuple-element.31.own_ref), channel_id=1, source_target_pairs={{0,4},{1,5},{2,6},{3,7},{4,0},{5,1},{6,2},{7,3},{8,12},{9,13},{10,... | collective-permute-start | bytes 1572872 | tf_op jit(solution)/shard_map/ppermute | solution.py:283
  111.2 1.2 copy-start.3
  112.4 1.0 copy-start.5
  113.4 9.8 %copy-start.8 = (f32[1056,128]{1,0:T(8,128)S(1)}, f32[1056,128]{1,0:T(8,128)}, u32[]{:S(2)}) copy-start(f32[1056,128]{1,0:T(8,128)} %copy-done.7) | copy-start | bytes 1622020
  113.4 9.8 %copy-start.10 = (f32[1024,128]{1,0:T(8,128)S(1)}, f32[1024,128]{1,0:T(8,128)}, u32[]{:S(2)}) copy-start(f32[1024,128]{1,0:T(8,128)} %copy-done.9) | copy-start | bytes 1572868
  113.4 9.8 %copy-start.12 = (f32[1024,128]{1,0:T(8,128)S(1)}, f32[1024,128]{1,0:T(8,128)}, u32[]{:S(2)}) copy-start(f32[1024,128]{1,0:T(8,128)} %copy-done.11) | copy-start | bytes 1572868

commit v4 on v3

--- a/solution.py
+++ b/solution.py
@@ -58,58 +58,92 @@
     return [(source == 2 * lane - shift).astype(jnp.bfloat16) for shift in (0, LANES)]
 
 
-def early_kernel(tail, who_ref, x_ref, gate_a_ref, gate_b_ref, mask_ref, part_ref, *pair_refs):
-    size = pair_refs[0].shape[1]
-    rows = size * len(pair_refs)
-    if tail:
-        mask = mask_ref[...].astype(jnp.float32).astype(jnp.bfloat16)
-        near, far = selectors()
-        part_ref[pl.ds(rows, tail)] = matmul(mask[:tail], near) + matmul(mask[tail:], far)
-    real, imag = gate_a_ref[0, 0], gate_a_ref[0, 1]
+def wide_gate(gate_ref, halves):
+    real, imag = gate_ref[0, 0], gate_ref[0, 1]
     pieces = []
-    for begin in (0, HALF):
+    for begin in range(0, halves * HALF, HALF):
         piece_real, piece_imag = real[begin : begin + HALF], imag[begin : begin + HALF]
         pieces.append(jnp.concatenate([piece_real, -piece_imag], axis=1))
         pieces.append(jnp.concatenate([piece_imag, piece_real], axis=1))
-    wide_high, wide_low = split_two(jnp.concatenate(pieces, axis=0))
+    return split_two(jnp.concatenate(pieces, axis=0))
+
+
+def first_kernel(who_ref, x_ref, gate_a_ref, gate_b_ref, mask_ref, part_ref):
+    tail = mask_ref.shape[0] // 2
+    rows = part_ref.shape[0] - tail
+    mask = mask_ref[...].astype(jnp.float32).astype(jnp.bfloat16)
+    near, far = selectors()
+    part_ref[pl.ds(rows, tail)] = matmul(mask[:tail], near) + matmul(mask[tail:], far)
     left = left_operand(gate_b_ref)
     value = jnp.concatenate([x_ref[part, 0].reshape(rows, LANES) for part in range(2)], axis=1)
-    value = right_gate(value, wide_high, wide_low)
+    value = right_gate(value, *wide_gate(gate_a_ref, 1))
+    for begin in range(0, rows, 2 * LANES):
+        both = [value[begin + side : begin + side + LANES] for side in (0, LANES)]
+        for side, piece in zip((0, LANES), left_gate(left, jnp.concatenate(both, axis=1))):
+            part_ref[pl.ds(begin + side, LANES)] = piece
+
+
+def early_kernel(sent, who_ref, x_ref, gate_a_ref, gate_b_ref, *refs):
+    pair_refs = refs[1:] if sent else refs
+    size = pair_refs[0].shape[1]
+    rows = size * len(pair_refs)
+    left = left_operand(gate_b_ref)
+    value = jnp.concatenate([x_ref[part, 0].reshape(rows, LANES) for part in range(2)], axis=1)
+    value = right_gate(value, *wide_gate(gate_a_ref, 2))
     for begin in range(0, rows, LANES):
         zero, one = left_gate(left, value[begin : begin + LANES])
-        part_ref[pl.ds(begin, LANES)] = zero
+        if sent:
+            refs[0][pl.ds(begin, LANES)] = zero
         pair_refs[begin // size][0, pl.ds(begin % size, LANES)] = zero
         pair_refs[begin // size][1, pl.ds(begin % size, LANES)] = one
 
 
-def early(who, x, gates, mask, apart, chunk, chunks, carrier, pieces):
-    blocks = x.shape[2] // chunks
-    rows = blocks * LANES
-    tail = mask.shape[0] // 2 if carrier else 0
+def apart_kernel(who_ref, x_ref, gate_a_ref, gate_b_ref, zero_ref, one_ref):
+    rows = zero_ref.shape[0]
+    left = left_operand(gate_b_ref)
+    value = jnp.concatenate([x_ref[part, 0].reshape(rows, LANES) for part in range(2)], axis=1)
+    value = right_gate(value, *wide_gate(gate_a_ref, 2))
+    for begin in range(0, rows, LANES):
+        place = pl.ds(begin, LANES)
+        zero_ref[place], one_ref[place] = left_gate(left, value[begin : begin + LANES])
+
+
+def early_call(kernel, who, x, gates, apart, shapes, *extra):
+    blocks = x.shape[2]
+
+    def whole(shape):
+        return pl.BlockSpec(shape, lambda g, who: (0,) * len(shape))
+
     return pl.pallas_call(
-        functools.partial(early_kernel, tail),
+        kernel,
         grid_spec=pltpu.PrefetchScalarGridSpec(
             num_scalar_prefetch=1,
             grid=(1,),
             in_specs=[
-                pl.BlockSpec((2, 1, blocks, LANES, LANES), lambda g, who: (0, who[0] ^ apart, chunk, 0, 0)),
+                pl.BlockSpec((2, 1, blocks, LANES, LANES), lambda g, who: (0, who[0] ^ apart, 0, 0, 0)),
                 pl.BlockSpec((1, 2, LANES, LANES), lambda g, who: (0, 0, 0, 0)),
                 pl.BlockSpec((1, 2, LANES, LANES), lambda g, who: (1, 0, 0, 0)),
-                pl.BlockSpec(mask.shape, lambda g, who: (0, 0)),
-            ],
-            out_specs=[
-                pl.BlockSpec((rows + tail, LANES), lambda g, who: (0, 0)),
             ]
-            + [pl.BlockSpec((2, rows // pieces, LANES), lambda g, who: (0, 0, 0))] * pieces,
+            + [whole(array.shape) for array in extra],
+            out_specs=[whole(shape) for shape in shapes],
         ),
-        out_shape=[
-            jax.ShapeDtypeStruct((rows + tail, LANES), jnp.float32),
-        ]
-        + [jax.ShapeDtypeStruct((2, rows // pieces, LANES), jnp.float32)] * pieces,
+        out_shape=[jax.ShapeDtypeStruct(shape, jnp.float32) for shape in shapes],
         compiler_params=pltpu.CompilerParams(vmem_limit_bytes=EARLY_LIMIT),
         cost_estimate=COST,
         name="early",
-    )(who, x, gates, gates, mask)
+    )(who, x, gates, gates, *extra)
+
+
+def early(who, x, gates, mask, apart, pieces):
+    rows = x.shape[2] * LANES
+    pairs = [(2, rows // pieces, LANES)] * pieces
+    if apart > 1:
+        return early_call(apart_kernel, who, x, gates, apart, [(rows, LANES)] * 2)
+    if apart:
+        return early_call(functools.partial(early_kernel, True), who, x, gates, apart, [(rows, LANES)] + pairs)
+    tail = mask.shape[0] // 2
+    part = early_call(first_kernel, who, x, gates, apart, [(rows + tail, LANES)], mask)
+    return part + early_call(functools.partial(early_kernel, False), who, x, gates, apart, pairs)
 
 
 def mix(coef_ref, at, value):
@@ -144,8 +178,8 @@
     else:
         control[...] = extra[0][...].astype(jnp.float32)
     for source, (apart, span, begin, rows) in zip(sources, places):
-        place = pl.ds(pl.multiple_of((who_ref[0] ^ apart) * span + begin, rows), rows)
-        held[place, :] = source[pl.ds(0, rows), :] if mixed else source[0]
+        place = pl.ds(pl.multiple_of((who_ref[0] ^ apart) * span + begin, LANES), rows)
+        held[place, :] = source[pl.ds(0, rows), :] if len(source.shape) == 2 else source[0]
 
     @pl.loop(0, stride // 4)
     def _(step):
@@ -195,7 +229,7 @@
     vmem = pl.BlockSpec(memory_space=pltpu.VMEM)
     smem = pl.BlockSpec(memory_space=pltpu.SMEM)
     source_specs = [
-        vmem if mixed else pl.BlockSpec((1, *source.shape[1:]), lambda g: (half, 0, 0)) for source in sources
+        vmem if source.ndim == 2 else pl.BlockSpec((1, *source.shape[1:]), lambda g: (half, 0, 0)) for source in sources
     ]
     gate_specs = [pl.BlockSpec((1, 2, LANES, LANES), lambda g, at=at: (at, 0, 0, 0)) for at in (2, 3)]
     return pl.pallas_call(
@@ -287,29 +321,26 @@
     span = total // groups
     ctrl = wide_ctrl(ctrl_gate)
     coefs = coefficients(mid_angles, parity)
-    away, away_places, pairs, pair_places = [], [], [], []
+    away, away_places, zeros, ones, places = [], [], [], [], []
     for apart in range(groups):
-        chunks = 1
-        pieces = 2 // chunks if apart == 1 and x.shape[2] % 2 == 0 else 1
-        size = span // chunks
-        for chunk in range(chunks):
-            carrier = apart == 0
-            part, *both = early(who, x, layer_gates, mask, apart, chunk, chunks, carrier, pieces)
-            away.append(move(part, apart))
-            away_places.append((apart, span, chunk * size, size))
-            for piece, pair in enumerate(both):
-                pairs.append(pair)
-                pair_places.append((apart, span, chunk * size + piece * (size // pieces), size // pieces))
-    first = [sent for sent, place in zip(away, away_places) if place[0] < 2]
-    for at, (apart, *_) in enumerate(pair_places):
+        pieces = 2 if apart == 1 and x.shape[2] % 2 == 0 else 1
+        part, *both = early(who, x, layer_gates, mask, apart, pieces)
+        away.append(move(part, apart))
+        away_places.append((apart, span, 0, span))
+        for piece, pair in enumerate(both):
+            ones.append(pair)
+            zeros.append(part if apart > 1 else pair)
+            places.append((apart, span, piece * (span // pieces), span // pieces))
+    for at, (apart, *_) in enumerate(places):
         if apart == 1:
-            pairs[at] = after(pairs[at], *first)
-        if apart:
-            pairs[at] = move(pairs[at], apart, 0)
+            zeros[at] = ones[at] = move(after(ones[at], *away[:2]), apart, 0)
+        elif apart:
+            zeros[at] = move(after(zeros[at], *away[:2]), apart, 0)
+            ones[at] = move(ones[at], apart, 0)
     sizes = [total // 8 * share for share in (2, 2, 2, 2)]
-    own_one = late(pairs, pair_places, layer_gates, ctrl, who, 1, sizes, mask)
+    own_one = late(ones, places, layer_gates, ctrl, who, 1, sizes, mask)
     other_one = [move(piece, 0) for piece in own_one]
-    (own_zero,) = late(pairs, pair_places, layer_gates, ctrl, who, 0, [total], mask)
+    (own_zero,) = late(zeros, places, layer_gates, ctrl, who, 0, [total], mask)
     (mixed,) = late(away, away_places, layer_gates, ctrl, who, 0, [total], own_zero, coefs)
     result = ()
     for at, size in enumerate(sizes):

time: 196 us -> 192 us (0.980)
  starting transfers between devices: 35 us -> 21.1 us
  local copies, waits for them, and re-layouts: 5.58 us -> 9.3 us
  waiting for transfers between devices: 90.3 us -> 93.9 us
  Pallas kernels: 58.9 us -> 61.7 us
    ppermute x12 -> x14, starting transfers between devices: 35 us -> 21.1 us  [move(): return lax.ppermute(value, ('high', 'mid'), pairs)]
    unnamed x30 -> x32, local copies, waits for them, and re-layouts: 4.84 us -> 8.59 us
    ppermute x12 -> x14, waiting for transfers between devices: 90.3 us -> 93.9 us  [move(): return lax.ppermute(value, ('high', 'mid'), pairs)]
    pallas_call x4 -> x5, Pallas kernels: 16.7 us -> 19.2 us  [early_call(): pl.pallas_call(kernel, grid_spec=pltpu.PrefetchScalarGridSpec(num_scalar_...]
  transfers between devices with their start and end apart: 12 -> 14, of which waited for: 7 -> 8; matrix products, arithmetic and copies ran while one was open for 0% -> 0% of each run, Pallas kernels for 27% -> 29%
where the time goes in v4:
time: 192 us; the launch traced here: 191 us
  waiting for transfers between devices  93.9 us (49%)
  Pallas kernels  61.7 us (32%)
  starting transfers between devices  21.1 us (11%)
  local copies, waits for them, and re-layouts  9.3 us (5%)
  between operations  5.15 us (3%)
    ppermute x14, waiting for transfers between devices, move(): return lax.ppermute(value, ('high', 'mid'), pairs)  93.9 us
    pallas_call x3, Pallas kernels, late(): pl.pallas_call(functools.partial(late_kernel, half, places, sizes, mixed)...  32.1 us
    ppermute x14, starting transfers between devices, move(): return lax.ppermute(value, ('high', 'mid'), pairs)  21.1 us
    pallas_call x5, Pallas kernels, early_call(): pl.pallas_call(kernel, grid_spec=pltpu.PrefetchScalarGridSpec(num_scalar_...  19.2 us
    pallas_call x4, Pallas kernels, final(): pl.pallas_call(final_kernel, grid=(rows // size,), in_specs=[pl.BlockSpec...  10.3 us
    unnamed x32, local copies, waits for them, and re-layouts  8.59 us
  transfers between devices with their start and end apart: 14, of which 8 were waited for; matrix products, arithmetic and copies ran while one was open for 0% of the time, Pallas kernels for 29%

profile of v4, /device:TPU:0, one launch (start us, length us, event | category | flops | bytes accessed | tf_op | source)
XLA Modules:
  0.0 191.3 jit_solution(17654831539341638480)
XLA Ops:
  0.0 3.2 %early.5 = f32[1056,128]{1,0:T(8,128)} custom-call(s32[1]{0:T(128)} %bitcast.who_ref.refs_8_.refs_7_, f32[2,4,8,128,128]{4,3,2,1,0:T(8,128)} %bitcast.17, f32[4,2,128,128]{3,2,1,0:T(8,128)} %refs_6_.3, f32[4,2,128,128]{3,2,1,0:T(8,128)} %refs_6_.3, s32[64,128]{1,0:T(8,128)} %bitcast.14), custom_call_target="tpu_custom_call" | custom-call | flops 1 | bytes 1 | tf_op jit(solution)/shard_map/early/pallas_call | solution.py:117
  3.2 4.0 %collective-permute-start = (f32[1056,128]{1,0:T(8,128)}, f32[1056,128]{1,0:T(8,128)S(1)}, u32[]{:S(2)}, u32[]{:S(2)}) collective-permute-start(f32[1056,128]{1,0:T(8,128)} %early.5), channel_id=1, source_target_pairs={{0,4},{1,5},{2,6},{3,7},{4,0},{5,1},{6,2},{7,3},{8,12},{9,13},{10,... | collective-permute-start | bytes 1622024 | tf_op jit(solution)/shard_map/ppermute | solution.py:317
  7.3 4.0 %early.6 = (f32[1024,128]{1,0:T(8,128)}, f32[2,512,128]{2,1,0:T(8,128)}, f32[2,512,128]{2,1,0:T(8,128)}) custom-call(s32[1]{0:T(128)} %bitcast.who_ref.refs_8_.refs_7_, f32[2,4,8,128,128]{4,3,2,1,0:T(8,128)} %bitcast.18, f32[4,2,128,128]{3,2,1,0:T(8,128)} %refs_6_.3, f32[4,2,128,128]{3,2,1,0:T(8,128)} %refs_6_.3), custom_call_target="tpu_custom_call" | custom-call | flops 1 | bytes 1 | tf_op jit(solution)/shard_map/early/pallas_call | solution.py:117
  11.3 4.0 %early.7 = (f32[1024,128]{1,0:T(8,128)}, f32[1024,128]{1,0:T(8,128)}) custom-call(s32[1]{0:T(128)} %bitcast.who_ref.refs_8_.refs_7_, f32[2,4,8,128,128]{4,3,2,1,0:T(8,128)} %bitcast.19, f32[4,2,128,128]{3,2,1,0:T(8,128)} %refs_6_.3, f32[4,2,128,128]{3,2,1,0:T(8,128)} %refs_6_.3), custom_call_target="tpu_custom_call" | custom-call | flops 1 | bytes 1 | tf_op jit(solution)/shard_map/early/pallas_call | solution.py:117
  15.3 1.5 collective-permute-start.8
  16.8 4.0 %early.8 = (f32[1024,128]{1,0:T(8,128)}, f32[1024,128]{1,0:T(8,128)}) custom-call(s32[1]{0:T(128)} %bitcast.who_ref.refs_8_.refs_7_, f32[2,4,8,128,128]{4,3,2,1,0:T(8,128)} %bitcast.20, f32[4,2,128,128]{3,2,1,0:T(8,128)} %refs_6_.3, f32[4,2,128,128]{3,2,1,0:T(8,128)} %refs_6_.3), custom_call_target="tpu_custom_call" | custom-call | flops 1 | bytes 1 | tf_op jit(solution)/shard_map/early/pallas_call | solution.py:117
  20.9 3.8 %collective-permute-start.2 = (f32[1024,128]{1,0:T(8,128)}, f32[1024,128]{1,0:T(8,128)}, u32[]{:S(2)}, u32[]{:S(2)}) collective-permute-start(f32[1024,128]{1,0:T(8,128)} %get-tuple-element.27), channel_id=1, source_target_pairs={{0,20},{1,21},{2,22},{3,23},{4,16},{5,17},{6,18},{7,19},{8,28},{9,... | collective-permute-start | bytes 1572872 | tf_op jit(solution)/shard_map/ppermute | solution.py:317
  24.7 4.0 %early.9.refs_0_ = f32[2,1024,128]{2,1,0:T(8,128)} custom-call(s32[1]{0:T(128)} %bitcast.who_ref.refs_8_.refs_7_, f32[2,4,8,128,128]{4,3,2,1,0:T(8,128)} %bitcast.21, f32[4,2,128,128]{3,2,1,0:T(8,128)} %refs_6_.3, f32[4,2,128,128]{3,2,1,0:T(8,128)} %refs_6_.3), custom_call_target="tpu_custom_call" | custom-call | flops 1 | bytes 1 | tf_op jit(solution)/shard_map/early/pallas_call | solution.py:117
  28.7 35.5 %collective-permute-done.1.refs_1_ = f32[1024,128]{1,0:T(8,128)S(1)} collective-permute-done((f32[1024,128]{1,0:T(8,128)}, f32[1024,128]{1,0:T(8,128)S(1)}, u32[]{:S(2)}, u32[]{:S(2)}) %collective-permute-start.1) | collective-permute-done | bytes 524320 | tf_op jit(solution)/shard_map/ppermute | solution.py:317
  64.2 1.5 collective-permute-start.4
  66.6 2.3 %collective-permute-start.6 = (f32[1024,128]{1,0:T(8,128)}, f32[1024,128]{1,0:T(8,128)S(1)}, u32[]{:S(2)}, u32[]{:S(2)}) collective-permute-start(f32[1024,128]{1,0:T(8,128)} %get-tuple-element.27), channel_id=1, source_target_pairs={{0,16},{1,17},{2,18},{3,19},{4,20},{5,21},{6,22},{7,23},{8,24},{9,... | collective-permute-start | bytes 1572872 | tf_op jit(solution)/shard_map/ppermute | solution.py:317
  69.8 1.1 collective-permute-start.3
  70.9 1.2 copy-done.1
  72.1 1.0 copy-done.10
  73.2 1.0 copy-done.12
  74.2 10.7 %late.5 = (f32[1024,128]{1,0:T(8,128)}, f32[1024,128]{1,0:T(8,128)}, f32[1024,128]{1,0:T(8,128)}, f32[1024,128]{1,0:T(8,128)}) custom-call(f32[2,1024,128]{2,1,0:T(8,128)S(1)} %copy-done.1, f32[2,512,128]{2,1,0:T(8,128)S(1)} %collective-permute-done.4.refs_1_, f32[2,512,128]{2,1,0:T(8,128)S(1)} %collective-permute-done.5.refs_2_, ...), custom_call_target="tpu_custom_call" | custom-call | flops 1 | bytes 1 | tf_op jit(solution)/shard_map/late/pallas_call | solution.py:235
  84.9 3.1 %collective-permute-start.13 = (f32[1024,128]{1,0:T(8,128)}, f32[1024,128]{1,0:T(8,128)}, u32[]{:S(2)}, u32[]{:S(2)}) collective-permute-start(f32[1024,128]{1,0:T(8,128)} %get-tuple-element.34.own_ref), channel_id=1, source_target_pairs={{0,4},{1,5},{2,6},{3,7},{4,0},{5,1},{6,2},{7,3},{8,12},{9,13},{10,... | collective-permute-start | bytes 1572872 | tf_op jit(solution)/shard_map/ppermute | solution.py:317
  88.0 1.9 collective-permute-done.2.refs_2_
  90.7 3.2 %collective-permute-start.11 = (f32[1024,128]{1,0:T(8,128)}, f32[1024,128]{1,0:T(8,128)}, u32[]{:S(2)}, u32[]{:S(2)}) collective-permute-start(f32[1024,128]{1,0:T(8,128)} %get-tuple-element.32.own_ref), channel_id=1, source_target_pairs={{0,4},{1,5},{2,6},{3,7},{4,0},{5,1},{6,2},{7,3},{8,12},{9,13},{10,... | collective-permute-start | bytes 1572872 | tf_op jit(solution)/shard_map/ppermute | solution.py:317
  93.9 8.6 %collective-permute-done.7.refs_4_ = f32[1024,128]{1,0:T(8,128)S(1)} collective-permute-done((f32[1024,128]{1,0:T(8,128)}, f32[1024,128]{1,0:T(8,128)S(1)}, u32[]{:S(2)}, u32[]{:S(2)}) %collective-permute-start.7) | collective-permute-done | bytes 524320 | tf_op jit(solution)/shard_map/ppermute | solution.py:317
  109.5 1.0 copy-done.6
  110.6 1.0 copy-done.8
  111.6 9.8 %late.3.refs_8_ = f32[4096,128]{1,0:T(8,128)S(1)} custom-call(f32[2,1024,128]{2,1,0:T(8,128)S(1)} %copy-done.2, f32[2,512,128]{2,1,0:T(8,128)S(1)} %collective-permute-done.4.refs_1_, f32[2,512,128]{2,1,0:T(8,128)S(1)} %collective-permute-done.5.refs_2_, f32[1024,128]{1,0:T(8,128)S(1)} %copy-done.6, f32[1024,128]{1,0:T(8,128)S(1)} %copy-done.8, ...), custom_call_target="tpu_custom_call" | custom-call | flops 1 | bytes 1 | tf_op jit(solution)/shard_map/late/pallas_call | solution.py:235
  121.4 22.3 %collective-permute-done.3.refs_3_ = f32[1024,128]{1,0:T(8,128)} collective-permute-done((f32[1024,128]{1,0:T(8,128)}, f32[1024,128]{1,0:T(8,128)}, u32[]{:S(2)}, u32[]{:S(2)}) %collective-permute-start.3) | collective-permute-done | bytes 524320 | tf_op jit(solution)/shard_map/ppermute | solution.py:317
  143.7 11.6 %late.4.zero_ref = f32[4096,128]{1,0:T(8,128)S(1)} custom-call(f32[1056,128]{1,0:T(8,128)S(1)} %collective-permute-done.refs_0_, f32[1024,128]{1,0:T(8,128)S(1)} %copy-done.4, f32[1024,128]{1,0:T(8,128)} %collective-permute-done.2.refs_2_, f32[1024,128]{1,0:T(8,128)} %collective-permute-done.3.refs_3_, f32[4,2,128,128]{3,2,1,0:T(8,128)S(1)} %copy-done, ...), custom_call_target="tpu_custom_call" | custom-call | flops 1 | bytes 1 | tf_op jit(solution)/shard_map/late/pallas_call | solution.py:235
  155.9 2.6 %final.4.refs_0_ = f32[2,4096,128]{2,1,0:T(8,128)} custom-call(f32[4096,128]{1,0:T(8,128)S(1)} %late.4.zero_ref, f32[1024,128]{1,0:T(8,128)} %get-tuple-element.34.own_ref, f32[1024,128]{1,0:T(8,128)} %collective-permute-done.13.other_ref, f32[4]{0:T(128)S(1)} %pad_maximum_fusion.refs_9_.coef_ref), custom_call_target="tpu_custom_call" | custom-call | flops 1 | bytes 1 | tf_op jit(solution)/shard_map/final/pallas_call | solution.py:267
  158.4 8.7 %collective-permute-done.12.other_ref = f32[1024,128]{1,0:T(8,128)} collective-permute-done((f32[1024,128]{1,0:T(8,128)}, f32[1024,128]{1,0:T(8,128)}, u32[]{:S(2)}, u32[]{:S(2)}) %collective-permute-start.12) | collective-permute-done | bytes 524320 | tf_op jit(solution)/shard_map/ppermute | solution.py:317
  167.1 2.6 %final.5.refs_0_ = f32[2,4096,128]{2,1,0:T(8,128)} custom-call(f32[4096,128]{1,0:T(8,128)S(1)} %late.4.zero_ref, f32[1024,128]{1,0:T(8,128)} %get-tuple-element.33.own_ref, f32[1024,128]{1,0:T(8,128)} %collective-permute-done.12.other_ref, f32[4]{0:T(128)S(1)} %pad_maximum_fusion.refs_9_.coef_ref, ...), custom_call_target="tpu_custom_call", output_to_operand_aliasing={{}: (4, {})} | custom-call | flops 1 | bytes 1 | tf_op jit(solution)/shard_map/final/pallas_call | solution.py:267
  169.7 8.7 %collective-permute-done.11.other_ref = f32[1024,128]{1,0:T(8,128)} collective-permute-done((f32[1024,128]{1,0:T(8,128)}, f32[1024,128]{1,0:T(8,128)}, u32[]{:S(2)}, u32[]{:S(2)}) %collective-permute-start.11) | collective-permute-done | bytes 524320 | tf_op jit(solution)/shard_map/ppermute | solution.py:317
  178.3 2.6 %final.6.refs_0_ = f32[2,4096,128]{2,1,0:T(8,128)} custom-call(f32[4096,128]{1,0:T(8,128)S(1)} %late.4.zero_ref, f32[1024,128]{1,0:T(8,128)} %get-tuple-element.32.own_ref, f32[1024,128]{1,0:T(8,128)} %collective-permute-done.11.other_ref, f32[4]{0:T(128)S(1)} %pad_maximum_fusion.refs_9_.coef_ref, ...), custom_call_target="tpu_custom_call", output_to_operand_aliasing={{}: (4, {})} | custom-call | flops 1 | bytes 1 | tf_op jit(solution)/shard_map/final/pallas_call | solution.py:267
  180.9 7.8 %collective-permute-done.10.other_ref = f32[1024,128]{1,0:T(8,128)} collective-permute-done((f32[1024,128]{1,0:T(8,128)}, f32[1024,128]{1,0:T(8,128)}, u32[]{:S(2)}, u32[]{:S(2)}) %collective-permute-start.10) | collective-permute-done | bytes 524320 | tf_op jit(solution)/shard_map/ppermute | solution.py:317
  188.7 2.6 %final.7 = f32[2,4096,128]{2,1,0:T(8,128)} custom-call(f32[4096,128]{1,0:T(8,128)S(1)} %late.4.zero_ref, f32[1024,128]{1,0:T(8,128)} %get-tuple-element.31.own_ref, f32[1024,128]{1,0:T(8,128)} %collective-permute-done.10.other_ref, f32[4]{0:T(128)S(1)} %pad_maximum_fusion.refs_9_.coef_ref, f32[2,4096,128]{2,1,0:T(8,128)} %final.6.refs_0_), custom_call_target="tpu_custom_call", output_to_operand_aliasing={{}: (4, {})} | custom-call | flops 1 | bytes 1 | tf_op jit(solution)/shard_map/final/pallas_call | solution.py:267
  (46 shorter events, 5.4 us)
Async XLA Ops:
  3.2 61.0 %collective-permute-start = (f32[1056,128]{1,0:T(8,128)}, f32[1056,128]{1,0:T(8,128)S(1)}, u32[]{:S(2)}, u32[]{:S(2)}) collective-permute-start(f32[1056,128]{1,0:T(8,128)} %early.5), channel_id=1, source_target_pairs={{0,4},{1,5},{2,6},{3,7},{4,0},{5,1},{6,2},{7,3},{8,12},{9,13},{10,... | collective-permute-start | bytes 1622024 | tf_op jit(solution)/shard_map/ppermute | solution.py:317
  11.3 52.9 %collective-permute-start.1 = (f32[1024,128]{1,0:T(8,128)}, f32[1024,128]{1,0:T(8,128)S(1)}, u32[]{:S(2)}, u32[]{:S(2)}) collective-permute-start(f32[1024,128]{1,0:T(8,128)} %get-tuple-element.20), channel_id=1, source_target_pairs={{0,12},{1,13},{2,14},{3,15},{4,8},{5,9},{6,10},{7,11},{8,4},{9,5},... | collective-permute-start | bytes 1572872 | tf_op jit(solution)/shard_map/ppermute | solution.py:317
  15.3 50.5 %collective-permute-start.8 = (f32[1024,128]{1,0:T(8,128)}, f32[1024,128]{1,0:T(8,128)S(1)}, u32[]{:S(2)}, u32[]{:S(2)}) collective-permute-start(f32[1024,128]{1,0:T(8,128)} %get-tuple-element.29), channel_id=1, source_target_pairs={{0,16},{1,17},{2,18},{3,19},{4,20},{5,21},{6,22},{7,23},{8,24},{9,... | collective-permute-start | bytes 1572872 | tf_op jit(solution)/shard_map/ppermute | solution.py:317
  20.8 48.9 %copy-start.14 = (f32[2,64,64]{2,1,0:T(8,128)S(1)}, f32[2,64,64]{2,1,0:T(8,128)}, u32[]{:S(2)}) copy-start(f32[2,64,64]{2,1,0:T(8,128)} %param.7) | copy-start | bytes 98308
  20.8 50.1 %copy-start = (f32[4,2,128,128]{3,2,1,0:T(8,128)S(1)}, f32[4,2,128,128]{3,2,1,0:T(8,128)}, u32[]{:S(2)}) copy-start(f32[4,2,128,128]{3,2,1,0:T(8,128)} %refs_6_.3) | copy-start | bytes 1572868
  20.8 50.1 %copy-start.13 = (s32[1,1,8192]{2,1,0:T(1,128)S(1)}, s32[1,1,8192]{2,1,0:T(1,128)}, u32[]{:S(2)}) copy-start(s32[1,1,8192]{2,1,0:T(1,128)} %param.8) | copy-start | bytes 98308
  20.8 48.0 %collective-permute-start.9 = (f32[1024,128]{1,0:T(8,128)}, f32[1024,128]{1,0:T(8,128)S(1)}, u32[]{:S(2)}, u32[]{:S(2)}) collective-permute-start(f32[1024,128]{1,0:T(8,128)} %get-tuple-element.30), channel_id=1, source_target_pairs={{0,24},{1,25},{2,26},{3,27},{4,28},{5,29},{6,30},{7,31},{8,16},{9,... | collective-permute-start | bytes 1572872 | tf_op jit(solution)/shard_map/ppermute | solution.py:317
  20.9 82.7 %copy-start.15 = (f32[3]{0:T(128)S(1)}, f32[3]{0:T(128)}, u32[]{:S(2)}) copy-start(f32[3]{0:T(128)} %param.9) | copy-start | bytes 40
  20.9 68.9 %collective-permute-start.2 = (f32[1024,128]{1,0:T(8,128)}, f32[1024,128]{1,0:T(8,128)}, u32[]{:S(2)}, u32[]{:S(2)}) collective-permute-start(f32[1024,128]{1,0:T(8,128)} %get-tuple-element.27), channel_id=1, source_target_pairs={{0,20},{1,21},{2,22},{3,23},{4,16},{5,17},{6,18},{7,19},{8,28},{9,... | collective-permute-start | bytes 1572872 | tf_op jit(solution)/shard_map/ppermute | solution.py:317
  64.2 20.7 %copy-start.3 = (f32[1024,128]{1,0:T(8,128)}, f32[1024,128]{1,0:T(8,128)S(1)}, u32[]{:S(2)}) copy-start(f32[1024,128]{1,0:T(8,128)S(1)} %collective-permute-done.1.refs_1_) | copy-start | bytes 1572868
  64.2 5.6 %collective-permute-start.4 = (f32[2,512,128]{2,1,0:T(8,128)}, f32[2,512,128]{2,1,0:T(8,128)S(1)}, u32[]{:S(2)}, u32[]{:S(2)}) collective-permute-start(f32[2,512,128]{2,1,0:T(8,128)} %get-tuple-element.24), channel_id=1, source_target_pairs={{0,8},{1,9},{2,10},{3,11},{4,12},{5,13},{6,14},{7,15},{8,0},{9,1},... | collective-permute-start | bytes 1572872 | tf_op jit(solution)/shard_map/ppermute | solution.py:317
  65.7 5.2 %collective-permute-start.5 = (f32[2,512,128]{2,1,0:T(8,128)}, f32[2,512,128]{2,1,0:T(8,128)S(1)}, u32[]{:S(2)}, u32[]{:S(2)}) collective-permute-start(f32[2,512,128]{2,1,0:T(8,128)} %get-tuple-element.26), channel_id=1, source_target_pairs={{0,8},{1,9},{2,10},{3,11},{4,12},{5,13},{6,14},{7,15},{8,0},{9,1},... | collective-permute-start | bytes 1572872 | tf_op jit(solution)/shard_map/ppermute | solution.py:317
  65.8 0.8 copy-start.9
  66.6 23.3 %collective-permute-start.6 = (f32[1024,128]{1,0:T(8,128)}, f32[1024,128]{1,0:T(8,128)S(1)}, u32[]{:S(2)}, u32[]{:S(2)}) collective-permute-start(f32[1024,128]{1,0:T(8,128)} %get-tuple-element.27), channel_id=1, source_target_pairs={{0,16},{1,17},{2,18},{3,19},{4,20},{5,21},{6,22},{7,23},{8,24},{9,... | collective-permute-start | bytes 1572872 | tf_op jit(solution)/shard_map/ppermute | solution.py:317
  68.8 0.8 copy-start.11
  69.7 32.8 %collective-permute-start.7 = (f32[1024,128]{1,0:T(8,128)}, f32[1024,128]{1,0:T(8,128)S(1)}, u32[]{:S(2)}, u32[]{:S(2)}) collective-permute-start(f32[1024,128]{1,0:T(8,128)} %get-tuple-element.28), channel_id=1, source_target_pairs={{0,24},{1,25},{2,26},{3,27},{4,28},{5,29},{6,30},{7,31},{8,16},{9,... | collective-permute-start | bytes 1572872 | tf_op jit(solution)/shard_map/ppermute | solution.py:317
  69.8 73.9 %collective-permute-start.3 = (f32[1024,128]{1,0:T(8,128)}, f32[1024,128]{1,0:T(8,128)}, u32[]{:S(2)}, u32[]{:S(2)}) collective-permute-start(f32[1024,128]{1,0:T(8,128)} %get-tuple-element.28), channel_id=1, source_target_pairs={{0,28},{1,29},{2,30},{3,31},{4,24},{5,25},{6,26},{7,27},{8,20},{9,... | collective-permute-start | bytes 1572872 | tf_op jit(solution)/shard_map/ppermute | solution.py:317
  70.9 1.2 copy-start.1
  72.1 1.0 copy-start.10
  73.2 1.0 copy-start.12
  74.2 35.3 %copy-start.2 = (f32[2,1024,128]{2,1,0:T(8,128)S(1)}, f32[2,1024,128]{2,1,0:T(8,128)}, u32[]{:S(2)}) copy-start(f32[2,1024,128]{2,1,0:T(8,128)} %early.9.refs_0_) | copy-start | bytes 3145732
  84.9 70.9 %collective-permute-start.13 = (f32[1024,128]{1,0:T(8,128)}, f32[1024,128]{1,0:T(8,128)}, u32[]{:S(2)}, u32[]{:S(2)}) collective-permute-start(f32[1024,128]{1,0:T(8,128)} %get-tuple-element.34.own_ref), channel_id=1, source_target_pairs={{0,4},{1,5},{2,6},{3,7},{4,0},{5,1},{6,2},{7,3},{8,12},{9,13},{10,... | collective-permute-start | bytes 1572872 | tf_op jit(solution)/shard_map/ppermute | solution.py:317
  89.9 77.2 %collective-permute-start.12 = (f32[1024,128]{1,0:T(8,128)}, f32[1024,128]{1,0:T(8,128)}, u32[]{:S(2)}, u32[]{:S(2)}) collective-permute-start(f32[1024,128]{1,0:T(8,128)} %get-tuple-element.33.own_ref), channel_id=1, source_target_pairs={{0,4},{1,5},{2,6},{3,7},{4,0},{5,1},{6,2},{7,3},{8,12},{9,13},{10,... | collective-permute-start | bytes 1572872 | tf_op jit(solution)/shard_map/ppermute | solution.py:317
  89.9 0.8 copy-start.5
  90.7 87.7 %collective-permute-start.11 = (f32[1024,128]{1,0:T(8,128)}, f32[1024,128]{1,0:T(8,128)}, u32[]{:S(2)}, u32[]{:S(2)}) collective-permute-start(f32[1024,128]{1,0:T(8,128)} %get-tuple-element.32.own_ref), channel_id=1, source_target_pairs={{0,4},{1,5},{2,6},{3,7},{4,0},{5,1},{6,2},{7,3},{8,12},{9,13},{10,... | collective-permute-start | bytes 1572872 | tf_op jit(solution)/shard_map/ppermute | solution.py:317
  102.4 0.8 copy-start.7
  103.2 85.5 %collective-permute-start.10 = (f32[1024,128]{1,0:T(8,128)}, f32[1024,128]{1,0:T(8,128)}, u32[]{:S(2)}, u32[]{:S(2)}) collective-permute-start(f32[1024,128]{1,0:T(8,128)} %get-tuple-element.31.own_ref), channel_id=1, source_target_pairs={{0,4},{1,5},{2,6},{3,7},{4,0},{5,1},{6,2},{7,3},{8,12},{9,13},{10,... | collective-permute-start | bytes 1572872 | tf_op jit(solution)/shard_map/ppermute | solution.py:317
  108.7 35.0 %copy-start.4 = (f32[1024,128]{1,0:T(8,128)S(1)}, f32[1024,128]{1,0:T(8,128)}, u32[]{:S(2)}) copy-start(f32[1024,128]{1,0:T(8,128)} %copy-done.3) | copy-start | bytes 1572868
  109.5 1.0 copy-start.6
  110.6 1.0 copy-start.8
